TPU v7x, 32 devices: a whole 2x2x4 slice. The times are simulated.
32 devices in a mesh: snap: 2 (over y), curve: 4 (over z), chan: 2 (over x), rep: 2 (over core).
Axes of the slice: x: 2, y: 2, z: 4, core: 2. Of those that a mesh axis runs over, the one named last changes fastest.
Arguments:
- children: bfloat16 [8, 128, 12288], P(None, None, ('snap', 'curve', 'rep')), parts along dimension 2, may hold values from -6 to 6
- child_mask: int32 [8, 12288], P(None, ('snap', 'curve', 'rep')), parts along dimension 1, may hold values from 0 to 1, as said below
- neighbours: int32 [27, 12288], P(None, ('snap', 'curve', 'rep')), parts along dimension 1, may hold values from -1 to 6143, as said below
- down_weight: bfloat16 [8, 256, 128], P(None, 'chan'), may hold values from -0.25 to 0.25
- conv_weight: bfloat16 [27, 256, 256], P(None, 'chan'), may hold values from -0.125 to 0.125
- cotangent: bfloat16 [256, 12288], P('chan', ('snap', 'curve', 'rep')), parts along dimension 1, may hold values from -6 to 6
Outputs:
- features_out: bfloat16 [256, 12288], P('chan', ('snap', 'curve', 'rep')), parts along dimension 1
- children_grad: bfloat16 [8, 128, 12288], P(None, 'chan', ('snap', 'curve', 'rep')), parts along dimension 2
- conv_weight_grad: float32 [54, 256, 256], P('snap', 'chan'), parts along dimension 0
- down_weight_grad: float32 [16, 256, 128], P('snap', 'chan'), parts along dimension 0
There are 2 independent parts, one for each index of `snap`. A program takes and returns all parts, laid end to end along the dimension named above; an argument that names none is the same for every part. Nothing has to cross between parts.
Inputs may be any that keep to these rules, and one draw needn't show every extreme that they name: Entry k of site p names the slot of the site at offset (k // 9 - 1, k // 3 % 3 - 1, k % 3 - 1) cells from p, or -1 where that cell is empty; entry 13 of an occupied site is p itself; neighbours[26 - k, neighbours[k, p]] = p wherever neighbours[k, p] >= 0; a site in slots j * 768 to (j + 1) * 768 - 1 names only sites in slots (j - 1) * 768 to (j + 2) * 768 - 1; empty slots hold -1 in all 27 entries. `child_mask`: 1 where the child cell is occupied; every occupied coarse site has at least one occupied child, empty slots have none.
All inputs are finite; a program needn't handle non-finite values.
Results may differ from a plain program's by a relative error of at most 0.0067.
Values may be sent and summed in bfloat16 or wider, within the bound.
No kernel may reach another device: no remote copies, remote signals or barrier semaphores. Data moves between devices by JAX's collectives and lax.ppermute only.
A program may use at most 128 MiB of HBM per device.

v0:
```python
import functools

import jax
import jax.numpy as jnp
from jax import lax
from jax.experimental import pallas as pl
from jax.experimental.pallas import tpu as pltpu
from jax.sharding import PartitionSpec as P

BLOCK = 128
SPAN = 256
GROUPS = 3
PER = 9
VMEM_LIMIT = 28 * 1024 * 1024
WHOLE_LIMIT = 60 * 1024 * 1024
PIECES = ("curve", "rep")
F32 = jnp.float32
BF16 = jnp.bfloat16
NOWHERE = -(2**20)
NT = (((1,), (1,)), ((), ()))


def silu_slope(value):
    sigma = jax.nn.sigmoid(value)
    return sigma * (1.0 + value * (1.0 - sigma))


def met(shard):
    devices = lax.axis_size(PIECES)
    pairs = [(i, i + 1) for i in range(1, devices - 1, 2)]
    pairs += [(j, i) for i, j in pairs]
    return [lax.ppermute(shard, PIECES, pairs), swapped(shard, "rep")]


def swapped(shard, axis):
    return lax.ppermute(shard, axis, [(0, 1), (1, 0)])


def call(kernel, out_shape, in_specs, scratch, out_specs=None, limit=VMEM_LIMIT):
    options = {} if out_specs is None else {"out_specs": out_specs}
    return pl.pallas_call(
        kernel,
        out_shape=out_shape,
        in_specs=in_specs,
        scratch_shapes=scratch,
        compiler_params=pltpu.CompilerParams(vmem_limit_bytes=limit),
        cost_estimate=pl.CostEstimate(flops=0, bytes_accessed=0, transcendentals=0),
        **options,
    )


def anywhere(count):
    return [pl.BlockSpec(memory_space=pl.ANY)] * count


def vmem(count):
    return [pl.BlockSpec(memory_space=pltpu.VMEM)] * count


SMEM = [pl.BlockSpec(memory_space=pltpu.SMEM)]


def down_kernel(children_ref, mask_ref, weight_ref, coarse_ref, slope_ref):
    octants = children_ref.shape[0]
    total = None
    for o in range(0, octants, 2):
        masked = jnp.concatenate(
            [
                children_ref[o + j] * mask_ref[o + j : o + j + 1, :].astype(F32).astype(BF16)
                for j in range(2)
            ],
            axis=0,
        )
        weights = jnp.concatenate([weight_ref[o], weight_ref[o + 1]], axis=1)
        term = jnp.dot(weights, masked, preferred_element_type=F32)
        total = term if total is None else total + term
    slope_ref[...] = silu_slope(total)
    coarse_ref[...] = (total * jax.nn.sigmoid(total)).T.astype(BF16)


def index_kernel(shards, neighbours_ref, index_ref, scalars_ref):
    offsets, rows = neighbours_ref.shape
    blocks = rows // BLOCK
    curve, rep = lax.axis_index("curve"), lax.axis_index("rep")
    names = neighbours_ref[...]
    local = jnp.where(names >= 0, names - (curve * 2 + rep - 1) * rows, NOWHERE)
    index_ref[...] = jnp.full(index_ref.shape, NOWHERE, jnp.int32)
    for group in range(GROUPS):
        part = local[group * PER : (group + 1) * PER]
        index_ref[group, :PER, :] = part
        lows = jnp.min(jnp.where(part < 0, -NOWHERE, part), axis=0, keepdims=True)
        highs = jnp.max(part, axis=0, keepdims=True)
        for block in range(blocks):
            at = slice(block * BLOCK, (block + 1) * BLOCK)
            low, high = jnp.min(lows[:, at]), jnp.max(highs[:, at]) + 1
            low = jnp.where(high <= 0, 0, low // 16 * 16)
            steps = jnp.maximum(1, (high - low + SPAN - 1) // SPAN)
            scalars_ref[group * blocks + block] = low
            scalars_ref[(GROUPS + group) * blocks + block] = steps
    last = 2 * GROUPS * blocks
    scalars_ref[last] = lax.axis_index("chan")
    scalars_ref[last + 1] = curve if shards > 1 else 0
    scalars_ref[last + 2] = rep


def fill_window(window_ref, parts, slots, rep):
    rows = parts[0][0].shape[0]
    places = (rows, rep * 2 * rows, (1 - rep) * 2 * rows)
    for part, slot in zip(parts, slots):
        for source, place in zip(part, places):
            window_ref[slot, pl.ds(pl.multiple_of(place, 16), rows), :] = source[...]
    blank = (window_ref.shape[0], window_ref.shape[1] - 3 * rows, window_ref.shape[2])
    window_ref[:, 3 * rows :, :] = jnp.zeros(blank, BF16)


def gather(scalars_ref, column_ref, window_ref, blocks, store, add):
    lanes = lax.broadcasted_iota(jnp.int32, (BLOCK, SPAN), 1).astype(F32).astype(BF16)

    def picked(group, rows, start):
        columns = jnp.clip(column_ref[group, rows, :] - start, -1, SPAN).astype(F32).astype(BF16)
        hot = [
            jnp.where(
                jnp.broadcast_to(columns[:, j : j + 1], (BLOCK, SPAN)) == lanes,
                jnp.ones((), BF16),
                jnp.zeros((), BF16),
            )
            for j in range(PER)
        ]
        at = pl.ds(pl.multiple_of(start, 16), SPAN)
        span = jnp.concatenate([window_ref[c, at, :] for c in range(window_ref.shape[0])], axis=1)
        return jnp.dot(jnp.concatenate(hot, axis=0), span, preferred_element_type=F32).astype(BF16)

    def first(block, _):
        rows = pl.ds(pl.multiple_of(block * BLOCK, BLOCK), BLOCK)
        for group in range(GROUPS):
            result = picked(group, rows, scalars_ref[group * blocks + block])
            for j in range(PER):
                store(group, j, rows, result[j * BLOCK : (j + 1) * BLOCK])
        return 0

    lax.fori_loop(0, blocks, first, 0, unroll=True)

    def rest(at, _):
        group, block = at // blocks, at % blocks
        rows = pl.ds(pl.multiple_of(block * BLOCK, BLOCK), BLOCK)

        def more(step, _):
            result = picked(group, rows, scalars_ref[at] + step * SPAN)
            for j in range(PER):
                add(group, j, rows, result[j * BLOCK : (j + 1) * BLOCK])
            return 0

        lax.fori_loop(1, scalars_ref[GROUPS * blocks + at], more, 0)
        return 0

    lax.fori_loop(0, GROUPS * blocks, rest, 0)


def turn(scratch_ref, value, shards, scalars_ref, at):
    half = value.shape[0] // 2
    size = half // shards
    scratch_ref[0] = value
    place = 0 if shards == 1 else scalars_ref[at + 1]
    rep = scalars_ref[at + 2]
    for core in range(2):
        for step in range(shards):
            source = (rep + core) % 2 * half + (place ^ step) * size
            target = core * half + step * size
            scratch_ref[1, target : target + size] = scratch_ref[
                0, pl.ds(pl.multiple_of(source, size), size)
            ]


def conv_kernel(chans, shards, scale, scalars_ref, index_ref, weight_ref, cotangent_ref, *refs):
    parts, refs = [refs[3 * i : 3 * i + 3] for i in range(chans)], refs[3 * chans :]
    out_ref, grad_ref, keep_ref, send_ref = refs[:4]
    window_ref, column_ref, picked_ref, conv_ref, scratch_ref = refs[4:]
    rows = index_ref.shape[2]
    blocks = rows // BLOCK
    width = chans * window_ref.shape[2]
    channels = weight_ref.shape[1]
    chan = scalars_ref[2 * GROUPS * blocks]
    rep = scalars_ref[2 * GROUPS * blocks + 2]
    slots = (chan, 1 - chan) if chans == 2 else range(chans)
    fill_window(window_ref, parts, slots, rep)
    for group in range(GROUPS):
        column_ref[group] = index_ref[group].T

    def store(group, j, at, value):
        lane = j % 3 * width
        picked_ref[group * 3 + j // 3, at, lane : lane + width] = value

    def add(group, j, at, value):
        lane = j % 3 * width
        picked_ref[group * 3 + j // 3, at, lane : lane + width] += value

    gather(scalars_ref, column_ref, window_ref, blocks, store, add)

    def multiply(three, _):
        weights = jnp.concatenate([weight_ref[three * 3 + j] for j in range(3)], axis=1)
        term = lax.dot_general(picked_ref[three], weights, NT, preferred_element_type=F32)
        conv_ref[...] += term
        return 0

    conv_ref[...] = jnp.zeros_like(conv_ref)
    lax.fori_loop(0, 9, multiply, 0, unroll=3)
    conv = conv_ref[...].T
    sigma = jax.nn.sigmoid(conv)
    out_ref[...] = (conv * sigma).astype(BF16)
    grad = cotangent_ref[...].astype(F32) * (sigma * (1.0 + conv * (1.0 - sigma)))
    grad_ref[...] = grad.T.astype(BF16)
    turn(scratch_ref, grad.astype(BF16), shards, scalars_ref, 2 * GROUPS * blocks)
    half = channels // 2
    size = half // shards

    def weigh(three, _):
        term = jnp.dot(scratch_ref[1], picked_ref[three], preferred_element_type=F32) * scale
        for j in range(3):
            both = term[:, j * width : (j + 1) * width].astype(BF16)
            for step in range(shards):
                at = step * size
                keep_ref[step, three * 3 + j] = both[at : at + size]
                send_ref[step, three * 3 + j] = both[half + at : half + at + size]
        return 0

    lax.fori_loop(0, 9, weigh, 0, unroll=3)


def coarse_grad_kernel(scalars_ref, index_ref, weight_ref, *refs):
    part, refs = refs[:3], refs[3:]
    mine_ref, other_ref, window_ref, column_ref, picked_ref, total_ref = refs
    rows = index_ref.shape[2]
    blocks = rows // BLOCK
    offsets, channels, width = weight_ref.shape
    chan = scalars_ref[2 * GROUPS * blocks]
    rep = scalars_ref[2 * GROUPS * blocks + 2]
    fill_window(window_ref, [part], (0,), rep)
    for group in range(GROUPS):
        column_ref[group] = index_ref[group].T

    def store(group, j, at, value):
        lane = (PER - 1 - j) * channels
        picked_ref[GROUPS - 1 - group, at, lane : lane + channels] = value

    def add(group, j, at, value):
        lane = (PER - 1 - j) * channels
        picked_ref[GROUPS - 1 - group, at, lane : lane + channels] += value

    gather(scalars_ref, column_ref, window_ref, blocks, store, add)
    result = None
    for group in range(GROUPS):
        weights = weight_ref[group * PER : (group + 1) * PER].reshape(PER * channels, width)
        term = jnp.dot(picked_ref[group], weights, preferred_element_type=F32)
        result = term if result is None else result + term
    result = result.T
    chans = width // channels
    for at in range(chans):
        total_ref[at] = result[at * channels : (at + 1) * channels]
    mine_ref[...] = total_ref[chan]
    for step in range(1, chans):
        other_ref[step - 1] = total_ref[lax.rem(chan + step, chans)].astype(BF16)


def pre_grad_kernel(scale, scalars_ref, children_ref, mask_ref, slope_ref, mine_ref, *refs):
    others, (grad_ref, keep_ref, send_ref, scratch_ref) = refs[:-4], refs[-4:]
    total = mine_ref[...]
    for other in others:
        total = total + other[...].astype(F32)
    grad = (total * slope_ref[...]).astype(BF16)
    grad_ref[...] = grad
    blocks = grad.shape[1] // BLOCK
    turn(scratch_ref, grad, 1, scalars_ref, 2 * GROUPS * blocks)
    half = grad.shape[0] // 2
    fine = children_ref.shape[1]
    for o in range(0, children_ref.shape[0], 2):
        masked = jnp.concatenate(
            [
                children_ref[o + j] * mask_ref[o + j : o + j + 1, :].astype(F32).astype(BF16)
                for j in range(2)
            ],
            axis=0,
        )
        term = lax.dot_general(scratch_ref[1], masked, NT, preferred_element_type=F32) * scale
        both = term.astype(BF16)
        for j in range(2):
            keep_ref[o + j] = both[:half, j * fine : (j + 1) * fine]
            send_ref[o + j] = both[half:, j * fine : (j + 1) * fine]


def cut_kernel(weight_ref, *refs):
    out_refs, scratch_ref = refs[:-1], refs[-1]
    octants, fine, _ = scratch_ref.shape
    chans = len(out_refs)
    size = fine // chans
    chan = lax.axis_index("chan")
    for o in range(octants):
        scratch_ref[o] = weight_ref[o].T
    for by in range(chans):
        at = pl.ds(pl.multiple_of((chan + by) % chans * size, size), size)
        for o in range(octants):
            out_refs[by][o] = scratch_ref[o, at, :]


def children_kernel(mask_ref, *refs):
    out_hbm, out_ref, sems = refs[-3:]
    count = (len(refs) - 3) // 2
    grads, weights = refs[:count], refs[count:-3]
    copies = []
    for o in range(out_ref.shape[0]):
        total = None
        for grad, weight in zip(grads, weights):
            term = jnp.dot(weight[o], grad[...], preferred_element_type=F32)
            term = term.astype(BF16).astype(F32)
            total = term if total is None else total + term
        out_ref[o] = (total * mask_ref[o : o + 1, :].astype(F32)).astype(BF16)
        copies.append(pltpu.make_async_copy(out_ref.at[o], out_hbm.at[o], sems.at[o]))
        copies[-1].start()
    for copy in copies:
        copy.wait()


def apart(shard, by):
    return lax.ppermute(shard, "curve", [(i, i ^ by) for i in range(lax.axis_size("curve"))])


def added(*terms):
    return sum(term.astype(F32) for term in terms).astype(BF16)


def after(value, *earlier):
    return lax.optimization_barrier((value, *earlier))[0]


def body(children, child_mask, neighbours, down_weight, conv_weight, cotangent):
    octants, fine, rows = children.shape
    offsets, channels, width = conv_weight.shape
    blocks = rows // BLOCK
    chans = lax.axis_size("chan")
    chan = lax.axis_index("chan")
    rep = lax.axis_index("rep")
    curve = lax.axis_index("curve")
    pieces = lax.axis_size(PIECES)
    scale = 1.0 / (rows * pieces) ** 0.5
    shape = jax.ShapeDtypeStruct
    half = channels // 2
    shards = 4 if lax.axis_size("curve") == 4 and half % 64 == 0 else 1
    size = half // shards

    coarse, slope = call(
        down_kernel,
        [shape((rows, channels), BF16), shape((channels, rows), F32)],
        vmem(3),
        [],
        limit=WHOLE_LIMIT,
    )(children, child_mask, down_weight)

    if chans == 2:
        parts = [coarse, swapped(coarse, "chan")]
    else:
        every = lax.all_gather(coarse, "chan", axis=0)
        parts = [every[i] for i in range(chans)]
    windows = [array for part in parts for array in [part] + met(part)]
    conv_weight = conv_weight * after(jnp.ones((), BF16), coarse)
    index, scalars = call(
        functools.partial(index_kernel, shards),
        [shape((GROUPS, 16, rows), jnp.int32), shape((2 * GROUPS * blocks + 3,), jnp.int32)],
        vmem(1),
        [],
        vmem(1) + SMEM,
    )(after(neighbours, parts[1]))

    features_out, conv_grad, keep, send = call(
        functools.partial(conv_kernel, chans, shards, scale),
        [
            shape((channels, rows), BF16),
            shape((rows, channels), BF16),
            shape((shards, offsets, size, width), BF16),
            shape((shards, offsets, size, width), BF16),
        ],
        SMEM + vmem(3 + 3 * chans),
        [
            pltpu.VMEM((chans, 3 * rows + SPAN, channels), BF16),
            pltpu.VMEM((GROUPS, rows, 16), jnp.int32),
            pltpu.VMEM((9, rows, 3 * width), BF16),
            pltpu.VMEM((rows, channels), F32),
            pltpu.VMEM((2, channels, rows), BF16),
        ],
    )(scalars, index, conv_weight, cotangent, *windows)

    near = met(conv_grad)
    received = swapped(send, "rep")
    total = [added(keep[i], received[i]) for i in range(shards)]
    terms = []
    if shards == 4:
        terms = [apart(after(total[by], near[1]), by) for by in (2, 3)]
        terms += [apart(total[1], 1)]

    mine, others = call(
        coarse_grad_kernel,
        [shape((channels, rows), F32), shape((chans - 1, channels, rows), BF16)],
        SMEM + vmem(5),
        [
            pltpu.VMEM((1, 3 * rows + SPAN, channels), BF16),
            pltpu.VMEM((GROUPS, rows, 16), jnp.int32),
            pltpu.VMEM((GROUPS, rows, PER * channels), BF16),
            pltpu.VMEM((chans, channels, rows), F32),
        ],
    )(after(scalars, *total), index, conv_weight, conv_grad, *near)
    received = [
        lax.ppermute(others[by - 1], "chan", [(i, (i + by) % chans) for i in range(chans)])
        for by in range(1, chans)
    ]
    mine_fine = fine // chans
    cut = call(
        cut_kernel,
        [shape((octants, mine_fine, channels), BF16)] * chans,
        vmem(1),
        [pltpu.VMEM((octants, fine, channels), BF16)],
    )(after(down_weight, mine))
    blank = [
        jnp.broadcast_to(after(jnp.zeros((), F32), mine), like.shape)
        for like in (conv_weight, down_weight)
    ]
    pre_grad, keep, send = call(
        functools.partial(pre_grad_kernel, scale),
        [
            shape((channels, rows), BF16),
            shape((octants, half, fine), BF16),
            shape((octants, half, fine), BF16),
        ],
        SMEM + vmem(4 + len(received)),
        [pltpu.VMEM((2, channels, rows), BF16)],
    )(after(scalars, *cut, *blank), children, child_mask, slope, mine, *received)

    if shards == 4:
        own = added(after(total[0], pre_grad), *terms)
    else:
        own = lax.psum(total[0], "curve")
    sent_grad, send = after(pre_grad, own), after(send, own)
    grads = [
        lax.ppermute(sent_grad, "chan", [(i, (i + by) % chans) for i in range(chans)])
        if by
        else pre_grad
        for by in range(chans)
    ]
    down = core_sum = added(keep, swapped(send, "rep"))
    sums = [own]
    if shards == 4:
        across = apart(own, 2)
        sums = [own, apart(own, 1), across, apart(across, 1)]
    if shards == 4:
        down = added(down, apart(down, 1))
    else:
        down = lax.psum(down, "curve")
    weights = [
        lax.ppermute(after(cut[by], own), "chan", [(i, (i + by) % chans) for i in range(chans)])
        if by
        else cut[by]
        for by in range(chans)
    ]
    children_grad = call(
        children_kernel,
        shape((octants, mine_fine, rows), BF16),
        vmem(1 + 2 * chans),
        [pltpu.VMEM((octants, mine_fine, rows), BF16), pltpu.SemaphoreType.DMA((octants,))],
        anywhere(1)[0],
    )(after(child_mask, down), *grads, *weights)
    if shards == 4:
        down = added(after(down, children_grad), apart(after(down, sums[2]), 2))

    def joined(result, pieces):
        for row, piece in pieces:
            result = lax.dynamic_update_slice(result, piece.astype(F32), (0, row, 0))
        return result

    rows_of = [rep * half, (1 - rep) * half]
    down_weight_grad = joined(blank[1], zip(rows_of, (down, swapped(down, "rep"))))
    pieces = []
    for step, part in enumerate(sums):
        at = (curve ^ step) * size if shards > 1 else 0
        mine = part if step else after(part, core_sum)
        pieces += [(rows_of[0] + at, mine), (rows_of[1] + at, swapped(part, "rep"))]
    conv_weight_grad = joined(blank[0], pieces)
    return (features_out, children_grad, conv_weight_grad, down_weight_grad)


def solution(mesh):
    in_specs = (
        P(None, None, ("snap", "curve", "rep")),
        P(None, ("snap", "curve", "rep")),
        P(None, ("snap", "curve", "rep")),
        P(None, "chan", None),
        P(None, "chan", None),
        P("chan", ("snap", "curve", "rep")),
    )
    out_specs = (
        P("chan", ("snap", "curve", "rep")),
        P(None, "chan", ("snap", "curve", "rep")),
        P("snap", "chan", None),
        P("snap", "chan", None),
    )
    return jax.shard_map(body, mesh=mesh, in_specs=in_specs, out_specs=out_specs, check_vma=False)
```

profile of v0, /device:TPU:0, one launch (start us, length us, event | category | flops | bytes accessed | tf_op | source)
XLA Modules:
  0.0 87.1 jit_solution(8755497167165787276)
XLA Ops:
  0.7 2.7 %shard_map.93 = (bf16[768,128]{1,0:T(8,128)(2,1)}, f32[128,768]{1,0:T(8,128)}) custom-call(bf16[8,128,768]{2,1,0:T(8,128)(2,1)} %children_ref.3, s32[8,768]{1,0:T(8,128)} %mask_ref.4, bf16[8,128,128]{2,1,0:T(8,128)(2,1)} %weight_ref.2), custom_call_target="tpu_custom_call" | custom-call | tf_op jit(solution)/shard_map/pallas_call | solution.py:349
  3.4 2.9 %collective-permute-start = (bf16[768,128]{1,0:T(8,128)(2,1)}, bf16[768,128]{1,0:T(8,128)(2,1)S(1)}, u32[]{:S(2)}, u32[]{:S(2)}) collective-permute-start(bf16[768,128]{1,0:T(8,128)(2,1)} %get-tuple-element.35.refs_0_), channel_id=1, source_target_pairs={{0,2},{2,0},{1,3},{3,1},{4,6},{6,4},{5,7},{7,5},{8,10},{10,8},{9,1... | collective-permute-start | bytes 589832 | tf_op jit(solution)/shard_map/ppermute | solution.py:36
  6.3 0.7 collective-permute-start.1
  7.0 3.0 %collective-permute-start.2 = (bf16[768,128]{1,0:T(8,128)(2,1)}, bf16[768,128]{1,0:T(8,128)(2,1)S(1)}, u32[]{:S(2)}, u32[]{:S(2)}) collective-permute-start(bf16[768,128]{1,0:T(8,128)(2,1)} %get-tuple-element.35.refs_0_), channel_id=1, source_target_pairs={{0,1},{1,0},{2,3},{3,2},{4,5},{5,4},{6,7},{7,6},{8,9},{9,8},{10,11... | collective-permute-start | bytes 589832 | tf_op jit(solution)/shard_map/ppermute | solution.py:36
  10.0 1.5 %collective-permute-done.refs_3_ = bf16[768,128]{1,0:T(8,128)(2,1)S(1)} collective-permute-done((bf16[768,128]{1,0:T(8,128)(2,1)}, bf16[768,128]{1,0:T(8,128)(2,1)S(1)}, u32[]{:S(2)}, u32[]{:S(2)}) %collective-permute-start) | collective-permute-done | bytes 196640 | tf_op jit(solution)/shard_map/ppermute | solution.py:36
  11.5 0.7 collective-permute-start.3
  12.2 3.2 %collective-permute-start.4 = (bf16[768,128]{1,0:T(8,128)(2,1)S(1)}, bf16[768,128]{1,0:T(8,128)(2,1)S(1)}, u32[]{:S(2)}, u32[]{:S(2)}) collective-permute-start(bf16[768,128]{1,0:T(8,128)(2,1)S(1)} %collective-permute-done.refs_3_), channel_id=1, source_target_pairs={{0,1},{1,0},{2,3},{3,2},{4,5},{5,4},{6,7},{7,6},{8,9},{9,8},{10,11... | collective-permute-start | bytes 589832 | tf_op jit(solution)/shard_map/ppermute | solution.py:36
  15.3 1.6 %broadcast_multiply_fusion.weight_ref = bf16[27,128,256]{2,1,0:T(8,128)(2,1)S(1)} fusion(bf16[27,128,256]{2,1,0:T(8,128)(2,1)} %param.10, bf16[]{:T(256)} %constant.3.clone.1), kind=kLoop, calls=%fused_computation | loop fusion | flops 884736 | bytes 3538946 | tf_op jit(solution)/shard_map/mul | solution.py:363
  17.0 1.0 %shard_map.94 = (s32[3,16,768]{2,1,0:T(8,128)S(1)}, s32[39]{0:T(128)S(1)}) custom-call(s32[27,768]{1,0:T(8,128)S(1)} %copy-done.6), custom_call_target="tpu_custom_call" | custom-call | tf_op jit(solution)/shard_map/pallas_call | solution.py:364
  18.1 10.0 %shard_map.95 = (bf16[128,768]{1,0:T(8,128)(2,1)}, bf16[768,128]{1,0:T(8,128)(2,1)S(1)}, bf16[4,27,16,256]{3,2,1,0:T(8,128)(2,1)S(1)}, bf16[4,27,16,256]{3,2,1,0:T(8,128)(2,1)S(1)}) custom-call(s32[39]{0:T(128)S(1)} %get-tuple-element.50.scalars_ref, s32[3,16,768]{2,1,0:T(8,128)S(1)} %get-tuple-element.38.index_ref, ...), custom_call_target="tpu_custom_call" | custom-call | tf_op jit(solution)/shard_map/pallas_call | solution.py:372
  28.1 0.6 collective-permute-start.5
  28.7 0.8 collective-permute-start.6
  29.6 3.9 %collective-permute-start.7 = (bf16[768,128]{1,0:T(8,128)(2,1)S(1)}, bf16[768,128]{1,0:T(8,128)(2,1)S(1)}, u32[]{:S(2)}, u32[]{:S(2)}) collective-permute-start(bf16[768,128]{1,0:T(8,128)(2,1)S(1)} %get-tuple-element.44.refs_0_), channel_id=1, source_target_pairs={{0,1},{1,0},{2,3},{3,2},{4,5},{5,4},{6,7},{7,6},{8,9},{9,8},{10,11... | collective-permute-start | bytes 589832 | tf_op jit(solution)/shard_map/ppermute | solution.py:36
  33.7 1.6 %collective-permute-start.11 = (bf16[27,16,256]{2,1,0:T(8,128)(2,1)S(1)}, bf16[27,16,256]{2,1,0:T(8,128)(2,1)S(1)}, u32[]{:S(2)}, u32[]{:S(2)}) collective-permute-start(bf16[27,16,256]{2,1,0:T(8,128)(2,1)S(1)} %get-tuple-element.70), channel_id=1, source_target_pairs={{0,4},{4,0},{8,12},{12,8},{1,5},{5,1},{9,13},{13,9},{2,6},{6,2},{1... | collective-permute-start | bytes 663560 | tf_op jit(solution)/shard_map/ppermute | solution.py:323
  35.3 2.1 %collective-permute-start.10 = (bf16[27,16,256]{2,1,0:T(8,128)(2,1)S(1)}, bf16[27,16,256]{2,1,0:T(8,128)(2,1)S(1)}, u32[]{:S(2)}, u32[]{:S(2)}) collective-permute-start(bf16[27,16,256]{2,1,0:T(8,128)(2,1)S(1)} %get-tuple-element.58), channel_id=1, source_target_pairs={{0,12},{4,8},{8,4},{12,0},{1,13},{5,9},{9,5},{13,1},{2,14},{6,10},... | collective-permute-start | bytes 663560 | tf_op jit(solution)/shard_map/ppermute | solution.py:323
  37.6 6.3 %shard_map.96 = (f32[128,768]{1,0:T(8,128)S(1)}, bf16[1,128,768]{2,1,0:T(8,128)(2,1)S(1)}) custom-call(s32[39]{0:T(128)S(1)} %get-tuple-element.50.scalars_ref, s32[3,16,768]{2,1,0:T(8,128)S(1)} %get-tuple-element.38.index_ref, bf16[27,128,256]{2,1,0:T(8,128)(2,1)S(1)} %broadcast_multiply_fusion.weight_ref, bf16[768,128]{1,0:T(8,128)(2,1)S(1)} %get-tuple-element.44.refs_0_, ...), custom_call_target="tpu_custom_call" | custom-call | tf_op jit(solution)/shard_map/pallas_call | solution.py:398
  43.9 1.6 %collective-permute-start.8 = (bf16[128,768]{1,0:T(8,128)(2,1)S(1)}, bf16[128,768]{1,0:T(8,128)(2,1)S(1)}, u32[]{:S(2)}, u32[]{:S(2)}) collective-permute-start(bf16[128,768]{1,0:T(8,128)(2,1)S(1)} %bitcast.9), channel_id=1, source_target_pairs={{0,2},{2,0},{1,3},{3,1},{4,6},{6,4},{5,7},{7,5},{8,10},{10,8},{9,1... | collective-permute-start | bytes 589832 | tf_op jit(solution)/shard_map/ppermute | solution.py:410
  45.6 5.0 %collective-permute-done.8.refs_0_ = bf16[128,768]{1,0:T(8,128)(2,1)S(1)} collective-permute-done((bf16[128,768]{1,0:T(8,128)(2,1)S(1)}, bf16[128,768]{1,0:T(8,128)(2,1)S(1)}, u32[]{:S(2)}, u32[]{:S(2)}) %collective-permute-start.8) | collective-permute-done | bytes 196640 | tf_op jit(solution)/shard_map/ppermute | solution.py:410
  50.6 1.2 %shard_map.98 = (bf16[128,768]{1,0:T(8,128)(2,1)S(1)}, bf16[8,64,128]{2,1,0:T(8,128)(2,1)S(1)}, bf16[8,64,128]{2,1,0:T(8,128)(2,1)S(1)}) custom-call(s32[39]{0:T(128)S(1)} %get-tuple-element.50.scalars_ref, bf16[8,128,768]{2,1,0:T(8,128)(2,1)S(1)} %copy-done, s32[8,768]{1,0:T(8,128)S(1)} %copy-done.3, f32[128,768]{1,0:T(8,128)S(1)} %copy-done.2, ...), custom_call_target="tpu_custom_call" | custom-call | tf_op jit(solution)/shard_map/pallas_call | solution.py:424
  51.8 5.7 %collective-permute-done.9 = bf16[27,16,256]{2,1,0:T(8,128)(2,1)S(1)} collective-permute-done((bf16[27,16,256]{2,1,0:T(8,128)(2,1)S(1)}, bf16[27,16,256]{2,1,0:T(8,128)(2,1)S(1)}, u32[]{:S(2)}, u32[]{:S(2)}) %collective-permute-start.9) | collective-permute-done | bytes 221216 | tf_op jit(solution)/shard_map/ppermute | solution.py:323
  58.2 2.7 %collective-permute-start.19 = (bf16[27,16,256]{2,1,0:T(8,128)(2,1)S(1)}, bf16[27,16,256]{2,1,0:T(8,128)(2,1)S(1)}, u32[]{:S(2)}, u32[]{:S(2)}) collective-permute-start(bf16[27,16,256]{2,1,0:T(8,128)(2,1)S(1)} %add_convert_fusion), channel_id=1, source_target_pairs={{0,8},{4,12},{8,0},{12,4},{1,9},{5,13},{9,1},{13,5},{2,10},{6,14},... | collective-permute-start | bytes 663560 | tf_op jit(solution)/shard_map/ppermute | solution.py:323
  60.9 1.5 %collective-permute-start.14 = (bf16[128,768]{1,0:T(8,128)(2,1)S(1)}, bf16[128,768]{1,0:T(8,128)(2,1)S(1)}, u32[]{:S(2)}, u32[]{:S(2)}) collective-permute-start(bf16[128,768]{1,0:T(8,128)(2,1)S(1)} %get-tuple-element.61.refs_0_), channel_id=1, source_target_pairs={{0,2},{2,0},{1,3},{3,1},{4,6},{6,4},{5,7},{7,5},{8,10},{10,8},{9,1... | collective-permute-start | bytes 589832 | tf_op jit(solution)/shard_map/ppermute | solution.py:441
  62.4 0.5 collective-permute-start.15
  63.5 7.5 %collective-permute-done.17 = bf16[27,16,256]{2,1,0:T(8,128)(2,1)S(1)} collective-permute-done((bf16[27,16,256]{2,1,0:T(8,128)(2,1)S(1)}, bf16[27,16,256]{2,1,0:T(8,128)(2,1)S(1)}, u32[]{:S(2)}, u32[]{:S(2)}) %collective-permute-start.17) | collective-permute-done | bytes 221216 | tf_op jit(solution)/shard_map/ppermute | solution.py:323
  71.5 1.6 %collective-permute-done.13 = bf16[8,64,128]{2,1,0:T(8,128)(2,1)S(1)} collective-permute-done((bf16[8,64,128]{2,1,0:T(8,128)(2,1)S(1)}, bf16[8,64,128]{2,1,0:T(8,128)(2,1)S(1)}, u32[]{:S(2)}, u32[]{:S(2)}) %collective-permute-start.13) | collective-permute-done | bytes 131104 | tf_op jit(solution)/shard_map/ppermute | solution.py:323
  73.2 1.1 %collective-permute-start.23 = (bf16[8,64,128]{2,1,0:T(8,128)(2,1)S(1)}, bf16[8,64,128]{2,1,0:T(8,128)(2,1)S(1)}, u32[]{:S(2)}, u32[]{:S(2)}) collective-permute-start(bf16[8,64,128]{2,1,0:T(8,128)(2,1)S(1)} %add_convert_fusion.6), channel_id=1, source_target_pairs={{0,8},{4,12},{8,0},{12,4},{1,9},{5,13},{9,1},{13,5},{2,10},{6,14},... | collective-permute-start | bytes 393224 | tf_op jit(solution)/shard_map/ppermute | solution.py:323
  74.4 1.8 %collective-permute-start.21 = (bf16[27,16,256]{2,1,0:T(8,128)(2,1)S(1)}, bf16[27,16,256]{2,1,0:T(8,128)(2,1)S(1)}, u32[]{:S(2)}, u32[]{:S(2)}) collective-permute-start(bf16[27,16,256]{2,1,0:T(8,128)(2,1)S(1)} %collective-permute-done.19), channel_id=1, source_target_pairs={{0,4},{4,0},{8,12},{12,8},{1,5},{5,1},{9,13},{13,9},{2,6},{6,2},{1... | collective-permute-start | bytes 663560 | tf_op jit(solution)/shard_map/ppermute | solution.py:323
  76.1 1.3 %shard_map.99 = bf16[8,64,768]{2,1,0:T(8,128)(2,1)} custom-call(s32[8,768]{1,0:T(8,128)S(1)} %copy-done.3, bf16[128,768]{1,0:T(8,128)(2,1)S(1)} %get-tuple-element.61.refs_0_, bf16[128,768]{1,0:T(8,128)(2,1)S(1)} %collective-permute-done.14.refs_1_, bf16[8,64,128]{2,1,0:T(8,128)(2,1)S(1)} %get-tuple-element.47.refs_2_, ...), custom_call_target="tpu_custom_call" | custom-call | tf_op jit(solution)/shard_map/pallas_call | solution.py:461
  77.4 4.4 %collective-permute-done.23 = bf16[8,64,128]{2,1,0:T(8,128)(2,1)S(1)} collective-permute-done((bf16[8,64,128]{2,1,0:T(8,128)(2,1)S(1)}, bf16[8,64,128]{2,1,0:T(8,128)(2,1)S(1)}, u32[]{:S(2)}, u32[]{:S(2)}) %collective-permute-start.23) | collective-permute-done | bytes 131104 | tf_op jit(solution)/shard_map/ppermute | solution.py:323
  82.0 1.7 %collective-permute-done.21 = bf16[27,16,256]{2,1,0:T(8,128)(2,1)S(1)} collective-permute-done((bf16[27,16,256]{2,1,0:T(8,128)(2,1)S(1)}, bf16[27,16,256]{2,1,0:T(8,128)(2,1)S(1)}, u32[]{:S(2)}, u32[]{:S(2)}) %collective-permute-start.21) | collective-permute-done | bytes 221216 | tf_op jit(solution)/shard_map/ppermute | solution.py:323
  84.0 1.2 %collective-permute-done.22 = bf16[27,16,256]{2,1,0:T(8,128)(2,1)S(1)} collective-permute-done((bf16[27,16,256]{2,1,0:T(8,128)(2,1)S(1)}, bf16[27,16,256]{2,1,0:T(8,128)(2,1)S(1)}, u32[]{:S(2)}, u32[]{:S(2)}) %collective-permute-start.22) | collective-permute-done | bytes 221216 | tf_op jit(solution)/shard_map/ppermute | solution.py:36
  85.3 1.8 %copy-done.7 = f32[27,128,256]{2,1,0:T(8,128)} copy-done((f32[27,128,256]{2,1,0:T(8,128)}, f32[27,128,256]{2,1,0:T(8,128)S(1)}, u32[]{:S(2)}) %copy-start.7) | copy-done | bytes 3538968
  (60 shorter events, 2.8 us)
Async XLA Ops:
  0.6 16.3 %copy-start.6 = (s32[27,768]{1,0:T(8,128)S(1)}, s32[27,768]{1,0:T(8,128)}, u32[]{:S(2)}) copy-start(s32[27,768]{1,0:T(8,128)} %neighbours_ref) | copy-start | bytes 248836
  0.6 17.4 %copy-start.4 = (bf16[128,768]{1,0:T(8,128)(2,1)S(1)}, bf16[128,768]{1,0:T(8,128)(2,1)}, u32[]{:S(2)}) copy-start(bf16[128,768]{1,0:T(8,128)(2,1)} %cotangent_ref.1) | copy-start | bytes 589828
  3.4 14.7 %copy-start.5 = (bf16[768,128]{1,0:T(8,128)(2,1)S(1)}, bf16[768,128]{1,0:T(8,128)(2,1)}, u32[]{:S(2)}) copy-start(bf16[768,128]{1,0:T(8,128)(2,1)} %get-tuple-element.35.refs_0_) | copy-start | bytes 589828
  3.4 8.1 %collective-permute-start = (bf16[768,128]{1,0:T(8,128)(2,1)}, bf16[768,128]{1,0:T(8,128)(2,1)S(1)}, u32[]{:S(2)}, u32[]{:S(2)}) collective-permute-start(bf16[768,128]{1,0:T(8,128)(2,1)} %get-tuple-element.35.refs_0_), channel_id=1, source_target_pairs={{0,2},{2,0},{1,3},{3,1},{4,6},{6,4},{5,7},{7,5},{8,10},{10,8},{9,1... | collective-permute-start | bytes 589832 | tf_op jit(solution)/shard_map/ppermute | solution.py:36
  6.3 11.7 %collective-permute-start.1 = (bf16[768,128]{1,0:T(8,128)(2,1)}, bf16[768,128]{1,0:T(8,128)(2,1)S(1)}, u32[]{:S(2)}, u32[]{:S(2)}) collective-permute-start(bf16[768,128]{1,0:T(8,128)(2,1)} %get-tuple-element.35.refs_0_), channel_id=1, source_target_pairs={{1,4},{5,8},{9,12},{4,1},{8,5},{12,9},{3,6},{7,10},{11,14},{6,3},{... | collective-permute-start | bytes 589832 | tf_op jit(solution)/shard_map/ppermute | solution.py:32
  7.0 11.0 %collective-permute-start.2 = (bf16[768,128]{1,0:T(8,128)(2,1)}, bf16[768,128]{1,0:T(8,128)(2,1)S(1)}, u32[]{:S(2)}, u32[]{:S(2)}) collective-permute-start(bf16[768,128]{1,0:T(8,128)(2,1)} %get-tuple-element.35.refs_0_), channel_id=1, source_target_pairs={{0,1},{1,0},{2,3},{3,2},{4,5},{5,4},{6,7},{7,6},{8,9},{9,8},{10,11... | collective-permute-start | bytes 589832 | tf_op jit(solution)/shard_map/ppermute | solution.py:36
  11.5 6.5 %collective-permute-start.3 = (bf16[768,128]{1,0:T(8,128)(2,1)S(1)}, bf16[768,128]{1,0:T(8,128)(2,1)S(1)}, u32[]{:S(2)}, u32[]{:S(2)}) collective-permute-start(bf16[768,128]{1,0:T(8,128)(2,1)S(1)} %collective-permute-done.refs_3_), channel_id=1, source_target_pairs={{1,4},{5,8},{9,12},{4,1},{8,5},{12,9},{3,6},{7,10},{11,14},{6,3},{... | collective-permute-start | bytes 589832 | tf_op jit(solution)/shard_map/ppermute | solution.py:32
  12.2 5.9 %collective-permute-start.4 = (bf16[768,128]{1,0:T(8,128)(2,1)S(1)}, bf16[768,128]{1,0:T(8,128)(2,1)S(1)}, u32[]{:S(2)}, u32[]{:S(2)}) collective-permute-start(bf16[768,128]{1,0:T(8,128)(2,1)S(1)} %collective-permute-done.refs_3_), channel_id=1, source_target_pairs={{0,1},{1,0},{2,3},{3,2},{4,5},{5,4},{6,7},{7,6},{8,9},{9,8},{10,11... | collective-permute-start | bytes 589832 | tf_op jit(solution)/shard_map/ppermute | solution.py:36
  18.1 27.3 %copy-start.1 = (bf16[8,128,128]{2,1,0:T(8,128)(2,1)S(1)}, bf16[8,128,128]{2,1,0:T(8,128)(2,1)}, u32[]{:S(2)}) copy-start(bf16[8,128,128]{2,1,0:T(8,128)(2,1)} %weight_ref.2) | copy-start | bytes 786436
  28.1 22.5 %copy-start = (bf16[8,128,768]{2,1,0:T(8,128)(2,1)S(1)}, bf16[8,128,768]{2,1,0:T(8,128)(2,1)}, u32[]{:S(2)}) copy-start(bf16[8,128,768]{2,1,0:T(8,128)(2,1)} %children_ref.3) | copy-start | bytes 4718596
  28.1 22.5 %copy-start.2 = (f32[128,768]{1,0:T(8,128)S(1)}, f32[128,768]{1,0:T(8,128)}, u32[]{:S(2)}) copy-start(f32[128,768]{1,0:T(8,128)} %get-tuple-element.51.slope_ref) | copy-start | bytes 1179652
  28.1 22.5 %copy-start.3 = (s32[8,768]{1,0:T(8,128)S(1)}, s32[8,768]{1,0:T(8,128)}, u32[]{:S(2)}) copy-start(s32[8,768]{1,0:T(8,128)} %mask_ref.4) | copy-start | bytes 73732
  28.1 5.4 %collective-permute-start.5 = (bf16[4,27,16,256]{3,2,1,0:T(8,128)(2,1)S(1)}, bf16[4,27,16,256]{3,2,1,0:T(8,128)(2,1)S(1)}, u32[]{:S(2)}, u32[]{:S(2)}) collective-permute-start(bf16[4,27,16,256]{3,2,1,0:T(8,128)(2,1)S(1)} %get-tuple-element.42), channel_id=1, source_target_pairs={{0,1},{1,0},{2,3},{3,2},{4,5},{5,4},{6,7},{7,6},{8,9},{9,8},{10,11... | collective-permute-start | bytes 2654216 | tf_op jit(solution)/shard_map/ppermute | solution.py:36
  28.7 8.9 %collective-permute-start.6 = (bf16[768,128]{1,0:T(8,128)(2,1)S(1)}, bf16[768,128]{1,0:T(8,128)(2,1)S(1)}, u32[]{:S(2)}, u32[]{:S(2)}) collective-permute-start(bf16[768,128]{1,0:T(8,128)(2,1)S(1)} %get-tuple-element.44.refs_0_), channel_id=1, source_target_pairs={{1,4},{5,8},{9,12},{4,1},{8,5},{12,9},{3,6},{7,10},{11,14},{6,3},{... | collective-permute-start | bytes 589832 | tf_op jit(solution)/shard_map/ppermute | solution.py:32
  29.6 5.8 %collective-permute-start.7 = (bf16[768,128]{1,0:T(8,128)(2,1)S(1)}, bf16[768,128]{1,0:T(8,128)(2,1)S(1)}, u32[]{:S(2)}, u32[]{:S(2)}) collective-permute-start(bf16[768,128]{1,0:T(8,128)(2,1)S(1)} %get-tuple-element.44.refs_0_), channel_id=1, source_target_pairs={{0,1},{1,0},{2,3},{3,2},{4,5},{5,4},{6,7},{7,6},{8,9},{9,8},{10,11... | collective-permute-start | bytes 589832 | tf_op jit(solution)/shard_map/ppermute | solution.py:36
  33.7 18.1 %collective-permute-start.11 = (bf16[27,16,256]{2,1,0:T(8,128)(2,1)S(1)}, bf16[27,16,256]{2,1,0:T(8,128)(2,1)S(1)}, u32[]{:S(2)}, u32[]{:S(2)}) collective-permute-start(bf16[27,16,256]{2,1,0:T(8,128)(2,1)S(1)} %get-tuple-element.70), channel_id=1, source_target_pairs={{0,4},{4,0},{8,12},{12,8},{1,5},{5,1},{9,13},{13,9},{2,6},{6,2},{1... | collective-permute-start | bytes 663560 | tf_op jit(solution)/shard_map/ppermute | solution.py:323
  35.3 16.4 %collective-permute-start.10 = (bf16[27,16,256]{2,1,0:T(8,128)(2,1)S(1)}, bf16[27,16,256]{2,1,0:T(8,128)(2,1)S(1)}, u32[]{:S(2)}, u32[]{:S(2)}) collective-permute-start(bf16[27,16,256]{2,1,0:T(8,128)(2,1)S(1)} %get-tuple-element.58), channel_id=1, source_target_pairs={{0,12},{4,8},{8,4},{12,0},{1,13},{5,9},{9,5},{13,1},{2,14},{6,10},... | collective-permute-start | bytes 663560 | tf_op jit(solution)/shard_map/ppermute | solution.py:323
  37.5 20.0 %collective-permute-start.9 = (bf16[27,16,256]{2,1,0:T(8,128)(2,1)S(1)}, bf16[27,16,256]{2,1,0:T(8,128)(2,1)S(1)}, u32[]{:S(2)}, u32[]{:S(2)}) collective-permute-start(bf16[27,16,256]{2,1,0:T(8,128)(2,1)S(1)} %get-tuple-element.57), channel_id=1, source_target_pairs={{0,8},{4,12},{8,0},{12,4},{1,9},{5,13},{9,1},{13,5},{2,10},{6,14},... | collective-permute-start | bytes 663560 | tf_op jit(solution)/shard_map/ppermute | solution.py:323
  43.9 6.7 %collective-permute-start.8 = (bf16[128,768]{1,0:T(8,128)(2,1)S(1)}, bf16[128,768]{1,0:T(8,128)(2,1)S(1)}, u32[]{:S(2)}, u32[]{:S(2)}) collective-permute-start(bf16[128,768]{1,0:T(8,128)(2,1)S(1)} %bitcast.9), channel_id=1, source_target_pairs={{0,2},{2,0},{1,3},{3,1},{4,6},{6,4},{5,7},{7,5},{8,10},{10,8},{9,1... | collective-permute-start | bytes 589832 | tf_op jit(solution)/shard_map/ppermute | solution.py:410
  57.6 4.8 %collective-permute-start.12 = (bf16[8,64,128]{2,1,0:T(8,128)(2,1)S(1)}, bf16[8,64,128]{2,1,0:T(8,128)(2,1)S(1)}, u32[]{:S(2)}, u32[]{:S(2)}) collective-permute-start(bf16[8,64,128]{2,1,0:T(8,128)(2,1)S(1)} %get-tuple-element.59), channel_id=1, source_target_pairs={{0,1},{1,0},{2,3},{3,2},{4,5},{5,4},{6,7},{7,6},{8,9},{9,8},{10,11... | collective-permute-start | bytes 393224 | tf_op jit(solution)/shard_map/ppermute | solution.py:36
  57.7 5.7 %collective-permute-start.16 = (bf16[27,16,256]{2,1,0:T(8,128)(2,1)S(1)}, bf16[27,16,256]{2,1,0:T(8,128)(2,1)S(1)}, u32[]{:S(2)}, u32[]{:S(2)}) collective-permute-start(bf16[27,16,256]{2,1,0:T(8,128)(2,1)S(1)} %add_convert_fusion), channel_id=1, source_target_pairs={{0,1},{1,0},{2,3},{3,2},{4,5},{5,4},{6,7},{7,6},{8,9},{9,8},{10,11... | collective-permute-start | bytes 663560 | tf_op jit(solution)/shard_map/ppermute | solution.py:36
  58.2 12.8 %collective-permute-start.17 = (bf16[27,16,256]{2,1,0:T(8,128)(2,1)S(1)}, bf16[27,16,256]{2,1,0:T(8,128)(2,1)S(1)}, u32[]{:S(2)}, u32[]{:S(2)}) collective-permute-start(bf16[27,16,256]{2,1,0:T(8,128)(2,1)S(1)} %add_convert_fusion), channel_id=1, source_target_pairs={{0,4},{4,0},{8,12},{12,8},{1,5},{5,1},{9,13},{13,9},{2,6},{6,2},{1... | collective-permute-start | bytes 663560 | tf_op jit(solution)/shard_map/ppermute | solution.py:323
  58.2 13.3 %collective-permute-start.19 = (bf16[27,16,256]{2,1,0:T(8,128)(2,1)S(1)}, bf16[27,16,256]{2,1,0:T(8,128)(2,1)S(1)}, u32[]{:S(2)}, u32[]{:S(2)}) collective-permute-start(bf16[27,16,256]{2,1,0:T(8,128)(2,1)S(1)} %add_convert_fusion), channel_id=1, source_target_pairs={{0,8},{4,12},{8,0},{12,4},{1,9},{5,13},{9,1},{13,5},{2,10},{6,14},... | collective-permute-start | bytes 663560 | tf_op jit(solution)/shard_map/ppermute | solution.py:323
  60.9 15.3 %collective-permute-start.14 = (bf16[128,768]{1,0:T(8,128)(2,1)S(1)}, bf16[128,768]{1,0:T(8,128)(2,1)S(1)}, u32[]{:S(2)}, u32[]{:S(2)}) collective-permute-start(bf16[128,768]{1,0:T(8,128)(2,1)S(1)} %get-tuple-element.61.refs_0_), channel_id=1, source_target_pairs={{0,2},{2,0},{1,3},{3,1},{4,6},{6,4},{5,7},{7,5},{8,10},{10,8},{9,1... | collective-permute-start | bytes 589832 | tf_op jit(solution)/shard_map/ppermute | solution.py:441
  62.4 12.0 %collective-permute-start.15 = (bf16[8,64,128]{2,1,0:T(8,128)(2,1)S(1)}, bf16[8,64,128]{2,1,0:T(8,128)(2,1)S(1)}, u32[]{:S(2)}, u32[]{:S(2)}) collective-permute-start(bf16[8,64,128]{2,1,0:T(8,128)(2,1)S(1)} %get-tuple-element.62), channel_id=1, source_target_pairs={{0,2},{2,0},{1,3},{3,1},{4,6},{6,4},{5,7},{7,5},{8,10},{10,8},{9,1... | collective-permute-start | bytes 393224 | tf_op jit(solution)/shard_map/ppermute | solution.py:456
  63.4 9.8 %collective-permute-start.13 = (bf16[8,64,128]{2,1,0:T(8,128)(2,1)S(1)}, bf16[8,64,128]{2,1,0:T(8,128)(2,1)S(1)}, u32[]{:S(2)}, u32[]{:S(2)}) collective-permute-start(bf16[8,64,128]{2,1,0:T(8,128)(2,1)S(1)} %add_convert_fusion.7), channel_id=1, source_target_pairs={{0,4},{4,0},{8,12},{12,8},{1,5},{5,1},{9,13},{13,9},{2,6},{6,2},{1... | collective-permute-start | bytes 393224 | tf_op jit(solution)/shard_map/ppermute | solution.py:323
  71.0 12.8 %collective-permute-start.18 = (bf16[27,16,256]{2,1,0:T(8,128)(2,1)S(1)}, bf16[27,16,256]{2,1,0:T(8,128)(2,1)S(1)}, u32[]{:S(2)}, u32[]{:S(2)}) collective-permute-start(bf16[27,16,256]{2,1,0:T(8,128)(2,1)S(1)} %collective-permute-done.17), channel_id=1, source_target_pairs={{0,1},{1,0},{2,3},{3,2},{4,5},{5,4},{6,7},{7,6},{8,9},{9,8},{10,11... | collective-permute-start | bytes 663560 | tf_op jit(solution)/shard_map/ppermute | solution.py:36
  71.4 12.4 %collective-permute-start.20 = (bf16[27,16,256]{2,1,0:T(8,128)(2,1)S(1)}, bf16[27,16,256]{2,1,0:T(8,128)(2,1)S(1)}, u32[]{:S(2)}, u32[]{:S(2)}) collective-permute-start(bf16[27,16,256]{2,1,0:T(8,128)(2,1)S(1)} %collective-permute-done.19), channel_id=1, source_target_pairs={{0,1},{1,0},{2,3},{3,2},{4,5},{5,4},{6,7},{7,6},{8,9},{9,8},{10,11... | collective-permute-start | bytes 663560 | tf_op jit(solution)/shard_map/ppermute | solution.py:36
  73.2 8.6 %collective-permute-start.23 = (bf16[8,64,128]{2,1,0:T(8,128)(2,1)S(1)}, bf16[8,64,128]{2,1,0:T(8,128)(2,1)S(1)}, u32[]{:S(2)}, u32[]{:S(2)}) collective-permute-start(bf16[8,64,128]{2,1,0:T(8,128)(2,1)S(1)} %add_convert_fusion.6), channel_id=1, source_target_pairs={{0,8},{4,12},{8,0},{12,4},{1,9},{5,13},{9,1},{13,5},{2,10},{6,14},... | collective-permute-start | bytes 393224 | tf_op jit(solution)/shard_map/ppermute | solution.py:323
  74.4 9.4 %collective-permute-start.21 = (bf16[27,16,256]{2,1,0:T(8,128)(2,1)S(1)}, bf16[27,16,256]{2,1,0:T(8,128)(2,1)S(1)}, u32[]{:S(2)}, u32[]{:S(2)}) collective-permute-start(bf16[27,16,256]{2,1,0:T(8,128)(2,1)S(1)} %collective-permute-done.19), channel_id=1, source_target_pairs={{0,4},{4,0},{8,12},{12,8},{1,5},{5,1},{9,13},{13,9},{2,6},{6,2},{1... | collective-permute-start | bytes 663560 | tf_op jit(solution)/shard_map/ppermute | solution.py:323
  81.9 2.0 %collective-permute-start.24 = (bf16[8,64,128]{2,1,0:T(8,128)(2,1)S(1)}, bf16[8,64,128]{2,1,0:T(8,128)(2,1)S(1)}, u32[]{:S(2)}, u32[]{:S(2)}) collective-permute-start(bf16[8,64,128]{2,1,0:T(8,128)(2,1)S(1)} %get-tuple-element.67), channel_id=1, source_target_pairs={{0,1},{1,0},{2,3},{3,2},{4,5},{5,4},{6,7},{7,6},{8,9},{9,8},{10,11... | collective-permute-start | bytes 393224 | tf_op jit(solution)/shard_map/ppermute | solution.py:36
  83.7 1.5 %collective-permute-start.22 = (bf16[27,16,256]{2,1,0:T(8,128)(2,1)S(1)}, bf16[27,16,256]{2,1,0:T(8,128)(2,1)S(1)}, u32[]{:S(2)}, u32[]{:S(2)}) collective-permute-start(bf16[27,16,256]{2,1,0:T(8,128)(2,1)S(1)} %collective-permute-done.21), channel_id=1, source_target_pairs={{0,1},{1,0},{2,3},{3,2},{4,5},{5,4},{6,7},{7,6},{8,9},{9,8},{10,11... | collective-permute-start | bytes 663560 | tf_op jit(solution)/shard_map/ppermute | solution.py:36
  (2 other events, 3.1 us)
where the time goes:
time: 87.2 us; the launch traced here: 87.1 us
  starting transfers between devices  29.5 us (34%)
  waiting for transfers between devices  29.1 us (33%)
  Pallas kernels  22.8 us (26%)
  other arithmetic  2.44 us (3%)
  local copies, waits for them, and re-layouts  2.24 us (3%)
  between operations  1.06 us (1%)
    ppermute x8, waiting for transfers between devices, apart(): lax.ppermute(shard, 'curve', [(i, i ^ by) for i in range(lax.axis_size('c...  21.4 us
    ppermute x11, starting transfers between devices, swapped(): return lax.ppermute(shard, axis, [(0, 1), (1, 0)])  14.3 us
    pallas_call x1, Pallas kernels, body(): call(functools.partial(conv_kernel, chans, shards, scale), [shape((channe...  10 us
    ppermute x8, starting transfers between devices, apart(): lax.ppermute(shard, 'curve', [(i, i ^ by) for i in range(lax.axis_size('c...  9.48 us
    pallas_call x1, Pallas kernels, body(): call(coarse_grad_kernel, [shape((channels, rows), F32), shape((chans - 1,...  6.28 us
    ppermute x1, waiting for transfers between devices, body(): lax.ppermute(others[by - 1], 'chan', [(i, (i + by) % chans) for i in rang...  4.96 us
    ppermute x11, waiting for transfers between devices, swapped(): return lax.ppermute(shard, axis, [(0, 1), (1, 0)])  2.74 us
    pallas_call x1, Pallas kernels, body(): call(down_kernel, [shape((rows, channels), BF16), shape((channels, rows),...  2.74 us
  transfers between devices with their start and end apart: 25, of which 9 were waited for; matrix products, arithmetic and copies ran while one was open for 3% of the time, Pallas kernels for 11%

commit v1 on v0

--- a/solution.py
+++ b/solution.py
@@ -25,11 +25,11 @@
     return sigma * (1.0 + value * (1.0 - sigma))
 
 
-def met(shard):
+def met(shard, later=None):
     devices = lax.axis_size(PIECES)
     pairs = [(i, i + 1) for i in range(1, devices - 1, 2)]
     pairs += [(j, i) for i, j in pairs]
-    return [lax.ppermute(shard, PIECES, pairs), swapped(shard, "rep")]
+    return [lax.ppermute(shard, PIECES, pairs), swapped(shard if later is None else later, "rep")]
 
 
 def swapped(shard, axis):
@@ -387,8 +387,8 @@
         ],
     )(scalars, index, conv_weight, cotangent, *windows)
 
-    near = met(conv_grad)
     received = swapped(send, "rep")
+    near = met(conv_grad, after(conv_grad, received))
     total = [added(keep[i], received[i]) for i in range(shards)]
     terms = []
     if shards == 4:
@@ -446,8 +446,7 @@
     down = core_sum = added(keep, swapped(send, "rep"))
     sums = [own]
     if shards == 4:
-        across = apart(own, 2)
-        sums = [own, apart(own, 1), across, apart(across, 1)]
+        sums = [own] + [apart(own, by) for by in range(1, 4)]
     if shards == 4:
         down = added(down, apart(down, 1))
     else:
@@ -466,7 +465,7 @@
         anywhere(1)[0],
     )(after(child_mask, down), *grads, *weights)
     if shards == 4:
-        down = added(after(down, children_grad), apart(after(down, sums[2]), 2))
+        down = added(after(down, children_grad), apart(down, 2))
 
     def joined(result, pieces):
         for row, piece in pieces:

time: 87.2 us -> 89.5 us (1.026)
  starting transfers between devices: 29.5 us -> 36.3 us
  waiting for transfers between devices: 29.1 us -> 26.3 us
  local copies, waits for them, and re-layouts: 2.24 us -> 1.33 us
    ppermute x8, starting transfers between devices: 9.48 us -> 15.8 us  [apart(): lax.ppermute(shard, 'curve', [(i, i ^ by) for i in range(lax.axis_size('c...]
    ppermute x8, waiting for transfers between devices: 21.4 us -> 16.4 us  [apart(): lax.ppermute(shard, 'curve', [(i, i ^ by) for i in range(lax.axis_size('c...]
    ppermute x11, waiting for transfers between devices: 2.74 us -> 3.78 us  [swapped(): return lax.ppermute(shard, axis, [(0, 1), (1, 0)])]
    ppermute x1, starting transfers between devices: 0.54 us -> 1.5 us  [body(): lax.ppermute(after(cut[by], own), 'chan', [(i, (i + by) % chans) for i in...]
    unnamed x18, local copies, waits for them, and re-layouts: 1.81 us -> 0.91 us
  transfers between devices with their start and end apart: 25 -> 25, of which waited for: 9 -> 8; matrix products, arithmetic and copies ran while one was open for 3% -> 3% of each run, Pallas kernels for 11% -> 11%
where the time goes in v1:
time: 89.5 us; the launch traced here: 89.4 us
  starting transfers between devices  36.3 us (41%)
  waiting for transfers between devices  26.3 us (29%)
  Pallas kernels  22 us (25%)
  other arithmetic  2.44 us (3%)
  local copies, waits for them, and re-layouts  1.33 us (1%)
  between operations  1.07 us (1%)
    ppermute x8, waiting for transfers between devices, apart(): lax.ppermute(shard, 'curve', [(i, i ^ by) for i in range(lax.axis_size('c...  16.4 us
    ppermute x8, starting transfers between devices, apart(): lax.ppermute(shard, 'curve', [(i, i ^ by) for i in range(lax.axis_size('c...  15.8 us
    ppermute x11, starting transfers between devices, swapped(): return lax.ppermute(shard, axis, [(0, 1), (1, 0)])  13.8 us
    pallas_call x1, Pallas kernels, body(): call(functools.partial(conv_kernel, chans, shards, scale), [shape((channe...  9.63 us
    pallas_call x1, Pallas kernels, body(): call(coarse_grad_kernel, [shape((channels, rows), F32), shape((chans - 1,...  5.92 us
    ppermute x1, waiting for transfers between devices, body(): lax.ppermute(others[by - 1], 'chan', [(i, (i + by) % chans) for i in rang...  5.3 us
    ppermute x11, waiting for transfers between devices, swapped(): return lax.ppermute(shard, axis, [(0, 1), (1, 0)])  3.78 us
    pallas_call x1, Pallas kernels, body(): call(down_kernel, [shape((rows, channels), BF16), shape((channels, rows),...  2.74 us
  transfers between devices with their start and end apart: 25, of which 8 were waited for; matrix products, arithmetic and copies ran while one was open for 3% of the time, Pallas kernels for 11%

profile of v1, /device:TPU:0, one launch (start us, length us, event | category | flops | bytes accessed | tf_op | source)
XLA Modules:
  0.0 89.4 jit_solution(696497065751312522)
XLA Ops:
  0.7 2.7 %shard_map.93 = (bf16[768,128]{1,0:T(8,128)(2,1)}, f32[128,768]{1,0:T(8,128)}) custom-call(bf16[8,128,768]{2,1,0:T(8,128)(2,1)} %children_ref.3, s32[8,768]{1,0:T(8,128)} %mask_ref.4, bf16[8,128,128]{2,1,0:T(8,128)(2,1)} %weight_ref.2), custom_call_target="tpu_custom_call" | custom-call | tf_op jit(solution)/shard_map/pallas_call | solution.py:349
  3.4 2.9 %collective-permute-start = (bf16[768,128]{1,0:T(8,128)(2,1)}, bf16[768,128]{1,0:T(8,128)(2,1)S(1)}, u32[]{:S(2)}, u32[]{:S(2)}) collective-permute-start(bf16[768,128]{1,0:T(8,128)(2,1)} %get-tuple-element.35.refs_0_), channel_id=1, source_target_pairs={{0,2},{2,0},{1,3},{3,1},{4,6},{6,4},{5,7},{7,5},{8,10},{10,8},{9,1... | collective-permute-start | bytes 589832 | tf_op jit(solution)/shard_map/ppermute | solution.py:36
  7.0 3.0 %collective-permute-start.2 = (bf16[768,128]{1,0:T(8,128)(2,1)}, bf16[768,128]{1,0:T(8,128)(2,1)S(1)}, u32[]{:S(2)}, u32[]{:S(2)}) collective-permute-start(bf16[768,128]{1,0:T(8,128)(2,1)} %get-tuple-element.35.refs_0_), channel_id=1, source_target_pairs={{0,1},{1,0},{2,3},{3,2},{4,5},{5,4},{6,7},{7,6},{8,9},{9,8},{10,11... | collective-permute-start | bytes 589832 | tf_op jit(solution)/shard_map/ppermute | solution.py:36
  10.0 1.5 %collective-permute-done.refs_3_ = bf16[768,128]{1,0:T(8,128)(2,1)S(1)} collective-permute-done((bf16[768,128]{1,0:T(8,128)(2,1)}, bf16[768,128]{1,0:T(8,128)(2,1)S(1)}, u32[]{:S(2)}, u32[]{:S(2)}) %collective-permute-start) | collective-permute-done | bytes 196640 | tf_op jit(solution)/shard_map/ppermute | solution.py:36
  12.2 3.2 %collective-permute-start.4 = (bf16[768,128]{1,0:T(8,128)(2,1)S(1)}, bf16[768,128]{1,0:T(8,128)(2,1)S(1)}, u32[]{:S(2)}, u32[]{:S(2)}) collective-permute-start(bf16[768,128]{1,0:T(8,128)(2,1)S(1)} %collective-permute-done.refs_3_), channel_id=1, source_target_pairs={{0,1},{1,0},{2,3},{3,2},{4,5},{5,4},{6,7},{7,6},{8,9},{9,8},{10,11... | collective-permute-start | bytes 589832 | tf_op jit(solution)/shard_map/ppermute | solution.py:36
  15.3 1.6 %broadcast_multiply_fusion.weight_ref = bf16[27,128,256]{2,1,0:T(8,128)(2,1)S(1)} fusion(bf16[27,128,256]{2,1,0:T(8,128)(2,1)} %param.10, bf16[]{:T(256)} %constant.3.clone.1), kind=kLoop, calls=%fused_computation | loop fusion | flops 884736 | bytes 3538946 | tf_op jit(solution)/shard_map/mul | solution.py:363
  17.0 1.0 %shard_map.94 = (s32[3,16,768]{2,1,0:T(8,128)S(1)}, s32[39]{0:T(128)S(1)}) custom-call(s32[27,768]{1,0:T(8,128)S(1)} %copy-done.6), custom_call_target="tpu_custom_call" | custom-call | tf_op jit(solution)/shard_map/pallas_call | solution.py:364
  18.1 9.6 %shard_map.95 = (bf16[128,768]{1,0:T(8,128)(2,1)}, bf16[768,128]{1,0:T(8,128)(2,1)S(1)}, bf16[4,27,16,256]{3,2,1,0:T(8,128)(2,1)S(1)}, bf16[4,27,16,256]{3,2,1,0:T(8,128)(2,1)S(1)}) custom-call(s32[39]{0:T(128)S(1)} %get-tuple-element.51.scalars_ref, s32[3,16,768]{2,1,0:T(8,128)S(1)} %get-tuple-element.38.index_ref, ...), custom_call_target="tpu_custom_call" | custom-call | tf_op jit(solution)/shard_map/pallas_call | solution.py:372
  27.7 1.0 %collective-permute-start.5 = (bf16[4,27,16,256]{3,2,1,0:T(8,128)(2,1)S(1)}, bf16[4,27,16,256]{3,2,1,0:T(8,128)(2,1)S(1)}, u32[]{:S(2)}, u32[]{:S(2)}) collective-permute-start(bf16[4,27,16,256]{3,2,1,0:T(8,128)(2,1)S(1)} %get-tuple-element.42), channel_id=1, source_target_pairs={{0,1},{1,0},{2,3},{3,2},{4,5},{5,4},{6,7},{7,6},{8,9},{9,8},{10,11... | collective-permute-start | bytes 2654216 | tf_op jit(solution)/shard_map/ppermute | solution.py:36
  28.7 0.8 collective-permute-start.6
  29.6 1.2 %collective-permute-done.5 = bf16[4,27,16,256]{3,2,1,0:T(8,128)(2,1)S(1)} collective-permute-done((bf16[4,27,16,256]{3,2,1,0:T(8,128)(2,1)S(1)}, bf16[4,27,16,256]{3,2,1,0:T(8,128)(2,1)S(1)}, u32[]{:S(2)}, u32[]{:S(2)}) %collective-permute-start.5) | collective-permute-done | bytes 884768 | tf_op jit(solution)/shard_map/ppermute | solution.py:36
  30.8 2.5 %collective-permute-start.7 = (bf16[768,128]{1,0:T(8,128)(2,1)S(1)}, bf16[768,128]{1,0:T(8,128)(2,1)S(1)}, u32[]{:S(2)}, u32[]{:S(2)}) collective-permute-start(bf16[768,128]{1,0:T(8,128)(2,1)S(1)} %get-tuple-element.45.refs_0_), channel_id=1, source_target_pairs={{0,1},{1,0},{2,3},{3,2},{4,5},{5,4},{6,7},{7,6},{8,9},{9,8},{10,11... | collective-permute-start | bytes 589832 | tf_op jit(solution)/shard_map/ppermute | solution.py:36
  33.5 2.0 %collective-permute-start.11 = (bf16[27,16,256]{2,1,0:T(8,128)(2,1)S(1)}, bf16[27,16,256]{2,1,0:T(8,128)(2,1)S(1)}, u32[]{:S(2)}, u32[]{:S(2)}) collective-permute-start(bf16[27,16,256]{2,1,0:T(8,128)(2,1)S(1)} %get-tuple-element.70), channel_id=1, source_target_pairs={{0,4},{4,0},{8,12},{12,8},{1,5},{5,1},{9,13},{13,9},{2,6},{6,2},{1... | collective-permute-start | bytes 663560 | tf_op jit(solution)/shard_map/ppermute | solution.py:323
  35.5 1.0 %collective-permute-start.9 = (bf16[27,16,256]{2,1,0:T(8,128)(2,1)S(1)}, bf16[27,16,256]{2,1,0:T(8,128)(2,1)S(1)}, u32[]{:S(2)}, u32[]{:S(2)}) collective-permute-start(bf16[27,16,256]{2,1,0:T(8,128)(2,1)S(1)} %get-tuple-element.58), channel_id=1, source_target_pairs={{0,8},{4,12},{8,0},{12,4},{1,9},{5,13},{9,1},{13,5},{2,10},{6,14},... | collective-permute-start | bytes 663560 | tf_op jit(solution)/shard_map/ppermute | solution.py:323
  36.5 2.1 %collective-permute-start.10 = (bf16[27,16,256]{2,1,0:T(8,128)(2,1)S(1)}, bf16[27,16,256]{2,1,0:T(8,128)(2,1)S(1)}, u32[]{:S(2)}, u32[]{:S(2)}) collective-permute-start(bf16[27,16,256]{2,1,0:T(8,128)(2,1)S(1)} %get-tuple-element.59), channel_id=1, source_target_pairs={{0,12},{4,8},{8,4},{12,0},{1,13},{5,9},{9,5},{13,1},{2,14},{6,10},... | collective-permute-start | bytes 663560 | tf_op jit(solution)/shard_map/ppermute | solution.py:323
  38.6 5.9 %shard_map.96 = (f32[128,768]{1,0:T(8,128)S(1)}, bf16[1,128,768]{2,1,0:T(8,128)(2,1)S(1)}) custom-call(s32[39]{0:T(128)S(1)} %get-tuple-element.51.scalars_ref, s32[3,16,768]{2,1,0:T(8,128)S(1)} %get-tuple-element.38.index_ref, bf16[27,128,256]{2,1,0:T(8,128)(2,1)S(1)} %broadcast_multiply_fusion.weight_ref, bf16[768,128]{1,0:T(8,128)(2,1)S(1)} %get-tuple-element.45.refs_0_, ...), custom_call_target="tpu_custom_call" | custom-call | tf_op jit(solution)/shard_map/pallas_call | solution.py:398
  44.5 1.6 %collective-permute-start.8 = (bf16[128,768]{1,0:T(8,128)(2,1)S(1)}, bf16[128,768]{1,0:T(8,128)(2,1)S(1)}, u32[]{:S(2)}, u32[]{:S(2)}) collective-permute-start(bf16[128,768]{1,0:T(8,128)(2,1)S(1)} %bitcast.9), channel_id=1, source_target_pairs={{0,2},{2,0},{1,3},{3,1},{4,6},{6,4},{5,7},{7,5},{8,10},{10,8},{9,1... | collective-permute-start | bytes 589832 | tf_op jit(solution)/shard_map/ppermute | solution.py:410
  46.3 5.3 %collective-permute-done.8.refs_0_ = bf16[128,768]{1,0:T(8,128)(2,1)S(1)} collective-permute-done((bf16[128,768]{1,0:T(8,128)(2,1)S(1)}, bf16[128,768]{1,0:T(8,128)(2,1)S(1)}, u32[]{:S(2)}, u32[]{:S(2)}) %collective-permute-start.8) | collective-permute-done | bytes 196640 | tf_op jit(solution)/shard_map/ppermute | solution.py:410
  51.6 1.2 %shard_map.98 = (bf16[128,768]{1,0:T(8,128)(2,1)S(1)}, bf16[8,64,128]{2,1,0:T(8,128)(2,1)S(1)}, bf16[8,64,128]{2,1,0:T(8,128)(2,1)S(1)}) custom-call(s32[39]{0:T(128)S(1)} %get-tuple-element.51.scalars_ref, bf16[8,128,768]{2,1,0:T(8,128)(2,1)S(1)} %copy-done, s32[8,768]{1,0:T(8,128)S(1)} %copy-done.3, f32[128,768]{1,0:T(8,128)S(1)} %copy-done.2, ...), custom_call_target="tpu_custom_call" | custom-call | tf_op jit(solution)/shard_map/pallas_call | solution.py:424
  52.8 1.4 %collective-permute-done.9 = bf16[27,16,256]{2,1,0:T(8,128)(2,1)S(1)} collective-permute-done((bf16[27,16,256]{2,1,0:T(8,128)(2,1)S(1)}, bf16[27,16,256]{2,1,0:T(8,128)(2,1)S(1)}, u32[]{:S(2)}, u32[]{:S(2)}) %collective-permute-start.9) | collective-permute-done | bytes 221216 | tf_op jit(solution)/shard_map/ppermute | solution.py:323
  54.9 4.1 %collective-permute-start.17 = (bf16[27,16,256]{2,1,0:T(8,128)(2,1)S(1)}, bf16[27,16,256]{2,1,0:T(8,128)(2,1)S(1)}, u32[]{:S(2)}, u32[]{:S(2)}) collective-permute-start(bf16[27,16,256]{2,1,0:T(8,128)(2,1)S(1)} %add_convert_fusion), channel_id=1, source_target_pairs={{0,4},{4,0},{8,12},{12,8},{1,5},{5,1},{9,13},{13,9},{2,6},{6,2},{1... | collective-permute-start | bytes 663560 | tf_op jit(solution)/shard_map/ppermute | solution.py:323
  59.5 1.9 %collective-permute-start.21 = (bf16[27,16,256]{2,1,0:T(8,128)(2,1)S(1)}, bf16[27,16,256]{2,1,0:T(8,128)(2,1)S(1)}, u32[]{:S(2)}, u32[]{:S(2)}) collective-permute-start(bf16[27,16,256]{2,1,0:T(8,128)(2,1)S(1)} %add_convert_fusion), channel_id=1, source_target_pairs={{0,12},{4,8},{8,4},{12,0},{1,13},{5,9},{9,5},{13,1},{2,14},{6,10},... | collective-permute-start | bytes 663560 | tf_op jit(solution)/shard_map/ppermute | solution.py:323
  61.3 1.5 %collective-permute-start.15 = (bf16[8,64,128]{2,1,0:T(8,128)(2,1)S(1)}, bf16[8,64,128]{2,1,0:T(8,128)(2,1)S(1)}, u32[]{:S(2)}, u32[]{:S(2)}) collective-permute-start(bf16[8,64,128]{2,1,0:T(8,128)(2,1)S(1)} %get-tuple-element.63), channel_id=1, source_target_pairs={{0,2},{2,0},{1,3},{3,1},{4,6},{6,4},{5,7},{7,5},{8,10},{10,8},{9,1... | collective-permute-start | bytes 393224 | tf_op jit(solution)/shard_map/ppermute | solution.py:455
  63.3 1.2 %collective-permute-start.13 = (bf16[8,64,128]{2,1,0:T(8,128)(2,1)S(1)}, bf16[8,64,128]{2,1,0:T(8,128)(2,1)S(1)}, u32[]{:S(2)}, u32[]{:S(2)}) collective-permute-start(bf16[8,64,128]{2,1,0:T(8,128)(2,1)S(1)} %add_convert_fusion.7), channel_id=1, source_target_pairs={{0,4},{4,0},{8,12},{12,8},{1,5},{5,1},{9,13},{13,9},{2,6},{6,2},{1... | collective-permute-start | bytes 393224 | tf_op jit(solution)/shard_map/ppermute | solution.py:323
  64.6 11.8 %collective-permute-done.13 = bf16[8,64,128]{2,1,0:T(8,128)(2,1)S(1)} collective-permute-done((bf16[8,64,128]{2,1,0:T(8,128)(2,1)S(1)}, bf16[8,64,128]{2,1,0:T(8,128)(2,1)S(1)}, u32[]{:S(2)}, u32[]{:S(2)}) %collective-permute-start.13) | collective-permute-done | bytes 131104 | tf_op jit(solution)/shard_map/ppermute | solution.py:323
  76.4 1.5 %collective-permute-start.14 = (bf16[128,768]{1,0:T(8,128)(2,1)S(1)}, bf16[128,768]{1,0:T(8,128)(2,1)S(1)}, u32[]{:S(2)}, u32[]{:S(2)}) collective-permute-start(bf16[128,768]{1,0:T(8,128)(2,1)S(1)} %get-tuple-element.62.refs_0_), channel_id=1, source_target_pairs={{0,2},{2,0},{1,3},{3,1},{4,6},{6,4},{5,7},{7,5},{8,10},{10,8},{9,1... | collective-permute-start | bytes 589832 | tf_op jit(solution)/shard_map/ppermute | solution.py:441
  77.9 3.0 %collective-permute-start.23 = (bf16[8,64,128]{2,1,0:T(8,128)(2,1)S(1)}, bf16[8,64,128]{2,1,0:T(8,128)(2,1)S(1)}, u32[]{:S(2)}, u32[]{:S(2)}) collective-permute-start(bf16[8,64,128]{2,1,0:T(8,128)(2,1)S(1)} %add_convert_fusion.6), channel_id=1, source_target_pairs={{0,8},{4,12},{8,0},{12,4},{1,9},{5,13},{9,1},{13,5},{2,10},{6,14},... | collective-permute-start | bytes 393224 | tf_op jit(solution)/shard_map/ppermute | solution.py:323
  81.7 0.8 collective-permute-done.14.refs_1_
  82.5 1.3 %shard_map.99 = bf16[8,64,768]{2,1,0:T(8,128)(2,1)} custom-call(s32[8,768]{1,0:T(8,128)S(1)} %copy-done.3, bf16[128,768]{1,0:T(8,128)(2,1)S(1)} %get-tuple-element.62.refs_0_, bf16[128,768]{1,0:T(8,128)(2,1)S(1)} %collective-permute-done.14.refs_1_, bf16[8,64,128]{2,1,0:T(8,128)(2,1)S(1)} %get-tuple-element.48.refs_2_, ...), custom_call_target="tpu_custom_call" | custom-call | tf_op jit(solution)/shard_map/pallas_call | solution.py:460
  83.8 3.2 %collective-permute-done.23 = bf16[8,64,128]{2,1,0:T(8,128)(2,1)S(1)} collective-permute-done((bf16[8,64,128]{2,1,0:T(8,128)(2,1)S(1)}, bf16[8,64,128]{2,1,0:T(8,128)(2,1)S(1)}, u32[]{:S(2)}, u32[]{:S(2)}) %collective-permute-start.23) | collective-permute-done | bytes 131104 | tf_op jit(solution)/shard_map/ppermute | solution.py:323
  87.5 1.0 %collective-permute-done.24 = bf16[8,64,128]{2,1,0:T(8,128)(2,1)S(1)} collective-permute-done((bf16[8,64,128]{2,1,0:T(8,128)(2,1)S(1)}, bf16[8,64,128]{2,1,0:T(8,128)(2,1)S(1)}, u32[]{:S(2)}, u32[]{:S(2)}) %collective-permute-start.24) | collective-permute-done | bytes 131104 | tf_op jit(solution)/shard_map/ppermute | solution.py:36
  88.5 0.7 copy-done.7
  (60 shorter events, 4.7 us)
Async XLA Ops:
  0.6 16.3 %copy-start.6 = (s32[27,768]{1,0:T(8,128)S(1)}, s32[27,768]{1,0:T(8,128)}, u32[]{:S(2)}) copy-start(s32[27,768]{1,0:T(8,128)} %neighbours_ref) | copy-start | bytes 248836
  0.6 17.4 %copy-start.4 = (bf16[128,768]{1,0:T(8,128)(2,1)S(1)}, bf16[128,768]{1,0:T(8,128)(2,1)}, u32[]{:S(2)}) copy-start(bf16[128,768]{1,0:T(8,128)(2,1)} %cotangent_ref.1) | copy-start | bytes 589828
  3.4 14.7 %copy-start.5 = (bf16[768,128]{1,0:T(8,128)(2,1)S(1)}, bf16[768,128]{1,0:T(8,128)(2,1)}, u32[]{:S(2)}) copy-start(bf16[768,128]{1,0:T(8,128)(2,1)} %get-tuple-element.35.refs_0_) | copy-start | bytes 589828
  3.4 8.1 %collective-permute-start = (bf16[768,128]{1,0:T(8,128)(2,1)}, bf16[768,128]{1,0:T(8,128)(2,1)S(1)}, u32[]{:S(2)}, u32[]{:S(2)}) collective-permute-start(bf16[768,128]{1,0:T(8,128)(2,1)} %get-tuple-element.35.refs_0_), channel_id=1, source_target_pairs={{0,2},{2,0},{1,3},{3,1},{4,6},{6,4},{5,7},{7,5},{8,10},{10,8},{9,1... | collective-permute-start | bytes 589832 | tf_op jit(solution)/shard_map/ppermute | solution.py:36
  6.3 11.7 %collective-permute-start.1 = (bf16[768,128]{1,0:T(8,128)(2,1)}, bf16[768,128]{1,0:T(8,128)(2,1)S(1)}, u32[]{:S(2)}, u32[]{:S(2)}) collective-permute-start(bf16[768,128]{1,0:T(8,128)(2,1)} %get-tuple-element.35.refs_0_), channel_id=1, source_target_pairs={{1,4},{5,8},{9,12},{4,1},{8,5},{12,9},{3,6},{7,10},{11,14},{6,3},{... | collective-permute-start | bytes 589832 | tf_op jit(solution)/shard_map/ppermute | solution.py:32
  7.0 11.0 %collective-permute-start.2 = (bf16[768,128]{1,0:T(8,128)(2,1)}, bf16[768,128]{1,0:T(8,128)(2,1)S(1)}, u32[]{:S(2)}, u32[]{:S(2)}) collective-permute-start(bf16[768,128]{1,0:T(8,128)(2,1)} %get-tuple-element.35.refs_0_), channel_id=1, source_target_pairs={{0,1},{1,0},{2,3},{3,2},{4,5},{5,4},{6,7},{7,6},{8,9},{9,8},{10,11... | collective-permute-start | bytes 589832 | tf_op jit(solution)/shard_map/ppermute | solution.py:36
  11.5 6.5 %collective-permute-start.3 = (bf16[768,128]{1,0:T(8,128)(2,1)S(1)}, bf16[768,128]{1,0:T(8,128)(2,1)S(1)}, u32[]{:S(2)}, u32[]{:S(2)}) collective-permute-start(bf16[768,128]{1,0:T(8,128)(2,1)S(1)} %collective-permute-done.refs_3_), channel_id=1, source_target_pairs={{1,4},{5,8},{9,12},{4,1},{8,5},{12,9},{3,6},{7,10},{11,14},{6,3},{... | collective-permute-start | bytes 589832 | tf_op jit(solution)/shard_map/ppermute | solution.py:32
  12.2 5.9 %collective-permute-start.4 = (bf16[768,128]{1,0:T(8,128)(2,1)S(1)}, bf16[768,128]{1,0:T(8,128)(2,1)S(1)}, u32[]{:S(2)}, u32[]{:S(2)}) collective-permute-start(bf16[768,128]{1,0:T(8,128)(2,1)S(1)} %collective-permute-done.refs_3_), channel_id=1, source_target_pairs={{0,1},{1,0},{2,3},{3,2},{4,5},{5,4},{6,7},{7,6},{8,9},{9,8},{10,11... | collective-permute-start | bytes 589832 | tf_op jit(solution)/shard_map/ppermute | solution.py:36
  18.1 28.0 %copy-start.1 = (bf16[8,128,128]{2,1,0:T(8,128)(2,1)S(1)}, bf16[8,128,128]{2,1,0:T(8,128)(2,1)}, u32[]{:S(2)}) copy-start(bf16[8,128,128]{2,1,0:T(8,128)(2,1)} %weight_ref.2) | copy-start | bytes 786436
  27.7 23.9 %copy-start = (bf16[8,128,768]{2,1,0:T(8,128)(2,1)S(1)}, bf16[8,128,768]{2,1,0:T(8,128)(2,1)}, u32[]{:S(2)}) copy-start(bf16[8,128,768]{2,1,0:T(8,128)(2,1)} %children_ref.3) | copy-start | bytes 4718596
  27.7 23.9 %copy-start.2 = (f32[128,768]{1,0:T(8,128)S(1)}, f32[128,768]{1,0:T(8,128)}, u32[]{:S(2)}) copy-start(f32[128,768]{1,0:T(8,128)} %get-tuple-element.52.slope_ref) | copy-start | bytes 1179652
  27.7 23.9 %copy-start.3 = (s32[8,768]{1,0:T(8,128)S(1)}, s32[8,768]{1,0:T(8,128)}, u32[]{:S(2)}) copy-start(s32[8,768]{1,0:T(8,128)} %mask_ref.4) | copy-start | bytes 73732
  27.7 3.0 %collective-permute-start.5 = (bf16[4,27,16,256]{3,2,1,0:T(8,128)(2,1)S(1)}, bf16[4,27,16,256]{3,2,1,0:T(8,128)(2,1)S(1)}, u32[]{:S(2)}, u32[]{:S(2)}) collective-permute-start(bf16[4,27,16,256]{3,2,1,0:T(8,128)(2,1)S(1)} %get-tuple-element.42), channel_id=1, source_target_pairs={{0,1},{1,0},{2,3},{3,2},{4,5},{5,4},{6,7},{7,6},{8,9},{9,8},{10,11... | collective-permute-start | bytes 2654216 | tf_op jit(solution)/shard_map/ppermute | solution.py:36
  28.7 9.9 %collective-permute-start.6 = (bf16[768,128]{1,0:T(8,128)(2,1)S(1)}, bf16[768,128]{1,0:T(8,128)(2,1)S(1)}, u32[]{:S(2)}, u32[]{:S(2)}) collective-permute-start(bf16[768,128]{1,0:T(8,128)(2,1)S(1)} %get-tuple-element.45.refs_0_), channel_id=1, source_target_pairs={{1,4},{5,8},{9,12},{4,1},{8,5},{12,9},{3,6},{7,10},{11,14},{6,3},{... | collective-permute-start | bytes 589832 | tf_op jit(solution)/shard_map/ppermute | solution.py:32
  30.8 4.7 %collective-permute-start.7 = (bf16[768,128]{1,0:T(8,128)(2,1)S(1)}, bf16[768,128]{1,0:T(8,128)(2,1)S(1)}, u32[]{:S(2)}, u32[]{:S(2)}) collective-permute-start(bf16[768,128]{1,0:T(8,128)(2,1)S(1)} %get-tuple-element.45.refs_0_), channel_id=1, source_target_pairs={{0,1},{1,0},{2,3},{3,2},{4,5},{5,4},{6,7},{7,6},{8,9},{9,8},{10,11... | collective-permute-start | bytes 589832 | tf_op jit(solution)/shard_map/ppermute | solution.py:36
  33.5 19.3 %collective-permute-start.11 = (bf16[27,16,256]{2,1,0:T(8,128)(2,1)S(1)}, bf16[27,16,256]{2,1,0:T(8,128)(2,1)S(1)}, u32[]{:S(2)}, u32[]{:S(2)}) collective-permute-start(bf16[27,16,256]{2,1,0:T(8,128)(2,1)S(1)} %get-tuple-element.70), channel_id=1, source_target_pairs={{0,4},{4,0},{8,12},{12,8},{1,5},{5,1},{9,13},{13,9},{2,6},{6,2},{1... | collective-permute-start | bytes 663560 | tf_op jit(solution)/shard_map/ppermute | solution.py:323
  35.5 18.7 %collective-permute-start.9 = (bf16[27,16,256]{2,1,0:T(8,128)(2,1)S(1)}, bf16[27,16,256]{2,1,0:T(8,128)(2,1)S(1)}, u32[]{:S(2)}, u32[]{:S(2)}) collective-permute-start(bf16[27,16,256]{2,1,0:T(8,128)(2,1)S(1)} %get-tuple-element.58), channel_id=1, source_target_pairs={{0,8},{4,12},{8,0},{12,4},{1,9},{5,13},{9,1},{13,5},{2,10},{6,14},... | collective-permute-start | bytes 663560 | tf_op jit(solution)/shard_map/ppermute | solution.py:323
  36.5 17.7 %collective-permute-start.10 = (bf16[27,16,256]{2,1,0:T(8,128)(2,1)S(1)}, bf16[27,16,256]{2,1,0:T(8,128)(2,1)S(1)}, u32[]{:S(2)}, u32[]{:S(2)}) collective-permute-start(bf16[27,16,256]{2,1,0:T(8,128)(2,1)S(1)} %get-tuple-element.59), channel_id=1, source_target_pairs={{0,12},{4,8},{8,4},{12,0},{1,13},{5,9},{9,5},{13,1},{2,14},{6,10},... | collective-permute-start | bytes 663560 | tf_op jit(solution)/shard_map/ppermute | solution.py:323
  44.5 7.0 %collective-permute-start.8 = (bf16[128,768]{1,0:T(8,128)(2,1)S(1)}, bf16[128,768]{1,0:T(8,128)(2,1)S(1)}, u32[]{:S(2)}, u32[]{:S(2)}) collective-permute-start(bf16[128,768]{1,0:T(8,128)(2,1)S(1)} %bitcast.9), channel_id=1, source_target_pairs={{0,2},{2,0},{1,3},{3,1},{4,6},{6,4},{5,7},{7,5},{8,10},{10,8},{9,1... | collective-permute-start | bytes 589832 | tf_op jit(solution)/shard_map/ppermute | solution.py:410
  54.3 7.0 %collective-permute-start.12 = (bf16[8,64,128]{2,1,0:T(8,128)(2,1)S(1)}, bf16[8,64,128]{2,1,0:T(8,128)(2,1)S(1)}, u32[]{:S(2)}, u32[]{:S(2)}) collective-permute-start(bf16[8,64,128]{2,1,0:T(8,128)(2,1)S(1)} %get-tuple-element.60), channel_id=1, source_target_pairs={{0,1},{1,0},{2,3},{3,2},{4,5},{5,4},{6,7},{7,6},{8,9},{9,8},{10,11... | collective-permute-start | bytes 393224 | tf_op jit(solution)/shard_map/ppermute | solution.py:36
  54.5 8.9 %collective-permute-start.16 = (bf16[27,16,256]{2,1,0:T(8,128)(2,1)S(1)}, bf16[27,16,256]{2,1,0:T(8,128)(2,1)S(1)}, u32[]{:S(2)}, u32[]{:S(2)}) collective-permute-start(bf16[27,16,256]{2,1,0:T(8,128)(2,1)S(1)} %add_convert_fusion), channel_id=1, source_target_pairs={{0,1},{1,0},{2,3},{3,2},{4,5},{5,4},{6,7},{7,6},{8,9},{9,8},{10,11... | collective-permute-start | bytes 663560 | tf_op jit(solution)/shard_map/ppermute | solution.py:36
  54.9 23.0 %collective-permute-start.17 = (bf16[27,16,256]{2,1,0:T(8,128)(2,1)S(1)}, bf16[27,16,256]{2,1,0:T(8,128)(2,1)S(1)}, u32[]{:S(2)}, u32[]{:S(2)}) collective-permute-start(bf16[27,16,256]{2,1,0:T(8,128)(2,1)S(1)} %add_convert_fusion), channel_id=1, source_target_pairs={{0,4},{4,0},{8,12},{12,8},{1,5},{5,1},{9,13},{13,9},{2,6},{6,2},{1... | collective-permute-start | bytes 663560 | tf_op jit(solution)/shard_map/ppermute | solution.py:323
  59.0 22.1 %collective-permute-start.19 = (bf16[27,16,256]{2,1,0:T(8,128)(2,1)S(1)}, bf16[27,16,256]{2,1,0:T(8,128)(2,1)S(1)}, u32[]{:S(2)}, u32[]{:S(2)}) collective-permute-start(bf16[27,16,256]{2,1,0:T(8,128)(2,1)S(1)} %add_convert_fusion), channel_id=1, source_target_pairs={{0,8},{4,12},{8,0},{12,4},{1,9},{5,13},{9,1},{13,5},{2,10},{6,14},... | collective-permute-start | bytes 663560 | tf_op jit(solution)/shard_map/ppermute | solution.py:323
  59.5 22.1 %collective-permute-start.21 = (bf16[27,16,256]{2,1,0:T(8,128)(2,1)S(1)}, bf16[27,16,256]{2,1,0:T(8,128)(2,1)S(1)}, u32[]{:S(2)}, u32[]{:S(2)}) collective-permute-start(bf16[27,16,256]{2,1,0:T(8,128)(2,1)S(1)} %add_convert_fusion), channel_id=1, source_target_pairs={{0,12},{4,8},{8,4},{12,0},{1,13},{5,9},{9,5},{13,1},{2,14},{6,10},... | collective-permute-start | bytes 663560 | tf_op jit(solution)/shard_map/ppermute | solution.py:323
  61.3 19.6 %collective-permute-start.15 = (bf16[8,64,128]{2,1,0:T(8,128)(2,1)S(1)}, bf16[8,64,128]{2,1,0:T(8,128)(2,1)S(1)}, u32[]{:S(2)}, u32[]{:S(2)}) collective-permute-start(bf16[8,64,128]{2,1,0:T(8,128)(2,1)S(1)} %get-tuple-element.63), channel_id=1, source_target_pairs={{0,2},{2,0},{1,3},{3,1},{4,6},{6,4},{5,7},{7,5},{8,10},{10,8},{9,1... | collective-permute-start | bytes 393224 | tf_op jit(solution)/shard_map/ppermute | solution.py:455
  63.3 13.0 %collective-permute-start.13 = (bf16[8,64,128]{2,1,0:T(8,128)(2,1)S(1)}, bf16[8,64,128]{2,1,0:T(8,128)(2,1)S(1)}, u32[]{:S(2)}, u32[]{:S(2)}) collective-permute-start(bf16[8,64,128]{2,1,0:T(8,128)(2,1)S(1)} %add_convert_fusion.7), channel_id=1, source_target_pairs={{0,4},{4,0},{8,12},{12,8},{1,5},{5,1},{9,13},{13,9},{2,6},{6,2},{1... | collective-permute-start | bytes 393224 | tf_op jit(solution)/shard_map/ppermute | solution.py:323
  76.4 6.1 %collective-permute-start.14 = (bf16[128,768]{1,0:T(8,128)(2,1)S(1)}, bf16[128,768]{1,0:T(8,128)(2,1)S(1)}, u32[]{:S(2)}, u32[]{:S(2)}) collective-permute-start(bf16[128,768]{1,0:T(8,128)(2,1)S(1)} %get-tuple-element.62.refs_0_), channel_id=1, source_target_pairs={{0,2},{2,0},{1,3},{3,1},{4,6},{6,4},{5,7},{7,5},{8,10},{10,8},{9,1... | collective-permute-start | bytes 589832 | tf_op jit(solution)/shard_map/ppermute | solution.py:441
  77.9 9.1 %collective-permute-start.23 = (bf16[8,64,128]{2,1,0:T(8,128)(2,1)S(1)}, bf16[8,64,128]{2,1,0:T(8,128)(2,1)S(1)}, u32[]{:S(2)}, u32[]{:S(2)}) collective-permute-start(bf16[8,64,128]{2,1,0:T(8,128)(2,1)S(1)} %add_convert_fusion.6), channel_id=1, source_target_pairs={{0,8},{4,12},{8,0},{12,4},{1,9},{5,13},{9,1},{13,5},{2,10},{6,14},... | collective-permute-start | bytes 393224 | tf_op jit(solution)/shard_map/ppermute | solution.py:323
  81.0 6.2 %collective-permute-start.18 = (bf16[27,16,256]{2,1,0:T(8,128)(2,1)S(1)}, bf16[27,16,256]{2,1,0:T(8,128)(2,1)S(1)}, u32[]{:S(2)}, u32[]{:S(2)}) collective-permute-start(bf16[27,16,256]{2,1,0:T(8,128)(2,1)S(1)} %collective-permute-done.17), channel_id=1, source_target_pairs={{0,1},{1,0},{2,3},{3,2},{4,5},{5,4},{6,7},{7,6},{8,9},{9,8},{10,11... | collective-permute-start | bytes 663560 | tf_op jit(solution)/shard_map/ppermute | solution.py:36
  81.1 6.2 %collective-permute-start.20 = (bf16[27,16,256]{2,1,0:T(8,128)(2,1)S(1)}, bf16[27,16,256]{2,1,0:T(8,128)(2,1)S(1)}, u32[]{:S(2)}, u32[]{:S(2)}) collective-permute-start(bf16[27,16,256]{2,1,0:T(8,128)(2,1)S(1)} %collective-permute-done.19), channel_id=1, source_target_pairs={{0,1},{1,0},{2,3},{3,2},{4,5},{5,4},{6,7},{7,6},{8,9},{9,8},{10,11... | collective-permute-start | bytes 663560 | tf_op jit(solution)/shard_map/ppermute | solution.py:36
  81.6 5.8 %collective-permute-start.22 = (bf16[27,16,256]{2,1,0:T(8,128)(2,1)S(1)}, bf16[27,16,256]{2,1,0:T(8,128)(2,1)S(1)}, u32[]{:S(2)}, u32[]{:S(2)}) collective-permute-start(bf16[27,16,256]{2,1,0:T(8,128)(2,1)S(1)} %collective-permute-done.21), channel_id=1, source_target_pairs={{0,1},{1,0},{2,3},{3,2},{4,5},{5,4},{6,7},{7,6},{8,9},{9,8},{10,11... | collective-permute-start | bytes 663560 | tf_op jit(solution)/shard_map/ppermute | solution.py:36
  87.1 1.4 %collective-permute-start.24 = (bf16[8,64,128]{2,1,0:T(8,128)(2,1)S(1)}, bf16[8,64,128]{2,1,0:T(8,128)(2,1)S(1)}, u32[]{:S(2)}, u32[]{:S(2)}) collective-permute-start(bf16[8,64,128]{2,1,0:T(8,128)(2,1)S(1)} %get-tuple-element.67), channel_id=1, source_target_pairs={{0,1},{1,0},{2,3},{3,2},{4,5},{5,4},{6,7},{7,6},{8,9},{9,8},{10,11... | collective-permute-start | bytes 393224 | tf_op jit(solution)/shard_map/ppermute | solution.py:36
  (2 other events, 2.7 us)

commit v2 on v0

--- a/solution.py
+++ b/solution.py
@@ -17,6 +17,7 @@
 F32 = jnp.float32
 BF16 = jnp.bfloat16
 NOWHERE = -(2**20)
+SHIFT = 2**16
 NT = (((1,), (1,)), ((), ()))
 
 
@@ -84,10 +85,13 @@
     curve, rep = lax.axis_index("curve"), lax.axis_index("rep")
     names = neighbours_ref[...]
     local = jnp.where(names >= 0, names - (curve * 2 + rep - 1) * rows, NOWHERE)
-    index_ref[...] = jnp.full(index_ref.shape, NOWHERE, jnp.int32)
+    last = 2 * GROUPS * blocks
+    found = 0
     for group in range(GROUPS):
         part = local[group * PER : (group + 1) * PER]
-        index_ref[group, :PER, :] = part
+        index_ref[group] = jnp.concatenate(
+            [part, jnp.full((16 - PER, rows), NOWHERE, jnp.int32)], axis=0
+        ).T
         lows = jnp.min(jnp.where(part < 0, -NOWHERE, part), axis=0, keepdims=True)
         highs = jnp.max(part, axis=0, keepdims=True)
         for block in range(blocks):
@@ -96,8 +100,13 @@
             low = jnp.where(high <= 0, 0, low // 16 * 16)
             steps = jnp.maximum(1, (high - low + SPAN - 1) // SPAN)
             scalars_ref[group * blocks + block] = low
-            scalars_ref[(GROUPS + group) * blocks + block] = steps
-    last = 2 * GROUPS * blocks
+
+            def note(step, found, at=group * blocks + block, low=low):
+                scalars_ref[last + 3 + found] = at * SHIFT + low + step * SPAN
+                return found + 1
+
+            found = lax.fori_loop(1, steps, note, found)
+    scalars_ref[GROUPS * blocks] = found
     scalars_ref[last] = lax.axis_index("chan")
     scalars_ref[last + 1] = curve if shards > 1 else 0
     scalars_ref[last + 2] = rep
@@ -140,20 +149,17 @@
 
     lax.fori_loop(0, blocks, first, 0, unroll=True)
 
-    def rest(at, _):
+    def rest(entry, _):
+        noted = scalars_ref[2 * GROUPS * blocks + 3 + entry]
+        at, start = noted // SHIFT, noted % SHIFT
         group, block = at // blocks, at % blocks
         rows = pl.ds(pl.multiple_of(block * BLOCK, BLOCK), BLOCK)
-
-        def more(step, _):
-            result = picked(group, rows, scalars_ref[at] + step * SPAN)
-            for j in range(PER):
-                add(group, j, rows, result[j * BLOCK : (j + 1) * BLOCK])
-            return 0
-
-        lax.fori_loop(1, scalars_ref[GROUPS * blocks + at], more, 0)
+        result = picked(group, rows, start)
+        for j in range(PER):
+            add(group, j, rows, result[j * BLOCK : (j + 1) * BLOCK])
         return 0
 
-    lax.fori_loop(0, GROUPS * blocks, rest, 0)
+    lax.fori_loop(0, scalars_ref[GROUPS * blocks], rest, 0)
 
 
 def turn(scratch_ref, value, shards, scalars_ref, at):
@@ -174,8 +180,8 @@
 def conv_kernel(chans, shards, scale, scalars_ref, index_ref, weight_ref, cotangent_ref, *refs):
     parts, refs = [refs[3 * i : 3 * i + 3] for i in range(chans)], refs[3 * chans :]
     out_ref, grad_ref, keep_ref, send_ref = refs[:4]
-    window_ref, column_ref, picked_ref, conv_ref, scratch_ref = refs[4:]
-    rows = index_ref.shape[2]
+    window_ref, picked_ref, conv_ref, scratch_ref = refs[4:]
+    rows = index_ref.shape[1]
     blocks = rows // BLOCK
     width = chans * window_ref.shape[2]
     channels = weight_ref.shape[1]
@@ -183,8 +189,6 @@
     rep = scalars_ref[2 * GROUPS * blocks + 2]
     slots = (chan, 1 - chan) if chans == 2 else range(chans)
     fill_window(window_ref, parts, slots, rep)
-    for group in range(GROUPS):
-        column_ref[group] = index_ref[group].T
 
     def store(group, j, at, value):
         lane = j % 3 * width
@@ -194,7 +198,7 @@
         lane = j % 3 * width
         picked_ref[group * 3 + j // 3, at, lane : lane + width] += value
 
-    gather(scalars_ref, column_ref, window_ref, blocks, store, add)
+    gather(scalars_ref, index_ref, window_ref, blocks, store, add)
 
     def multiply(three, _):
         weights = jnp.concatenate([weight_ref[three * 3 + j] for j in range(3)], axis=1)
@@ -228,15 +232,13 @@
 
 def coarse_grad_kernel(scalars_ref, index_ref, weight_ref, *refs):
     part, refs = refs[:3], refs[3:]
-    mine_ref, other_ref, window_ref, column_ref, picked_ref, total_ref = refs
-    rows = index_ref.shape[2]
+    mine_ref, other_ref, window_ref, picked_ref, total_ref = refs
+    rows = index_ref.shape[1]
     blocks = rows // BLOCK
     offsets, channels, width = weight_ref.shape
     chan = scalars_ref[2 * GROUPS * blocks]
     rep = scalars_ref[2 * GROUPS * blocks + 2]
     fill_window(window_ref, [part], (0,), rep)
-    for group in range(GROUPS):
-        column_ref[group] = index_ref[group].T
 
     def store(group, j, at, value):
         lane = (PER - 1 - j) * channels
@@ -246,7 +248,7 @@
         lane = (PER - 1 - j) * channels
         picked_ref[GROUPS - 1 - group, at, lane : lane + channels] += value
 
-    gather(scalars_ref, column_ref, window_ref, blocks, store, add)
+    gather(scalars_ref, index_ref, window_ref, blocks, store, add)
     result = None
     for group in range(GROUPS):
         weights = weight_ref[group * PER : (group + 1) * PER].reshape(PER * channels, width)
@@ -361,9 +363,10 @@
         parts = [every[i] for i in range(chans)]
     windows = [array for part in parts for array in [part] + met(part)]
     conv_weight = conv_weight * after(jnp.ones((), BF16), coarse)
+    listed = GROUPS * blocks * (3 * rows // SPAN)
     index, scalars = call(
         functools.partial(index_kernel, shards),
-        [shape((GROUPS, 16, rows), jnp.int32), shape((2 * GROUPS * blocks + 3,), jnp.int32)],
+        [shape((GROUPS, rows, 16), jnp.int32), shape((2 * GROUPS * blocks + 3 + listed,), jnp.int32)],
         vmem(1),
         [],
         vmem(1) + SMEM,
@@ -380,7 +383,6 @@
         SMEM + vmem(3 + 3 * chans),
         [
             pltpu.VMEM((chans, 3 * rows + SPAN, channels), BF16),
-            pltpu.VMEM((GROUPS, rows, 16), jnp.int32),
             pltpu.VMEM((9, rows, 3 * width), BF16),
             pltpu.VMEM((rows, channels), F32),
             pltpu.VMEM((2, channels, rows), BF16),
@@ -401,7 +403,6 @@
         SMEM + vmem(5),
         [
             pltpu.VMEM((1, 3 * rows + SPAN, channels), BF16),
-            pltpu.VMEM((GROUPS, rows, 16), jnp.int32),
             pltpu.VMEM((GROUPS, rows, PER * channels), BF16),
             pltpu.VMEM((chans, channels, rows), F32),
         ],

time: 87.2 us -> 89 us (1.021)
  Pallas kernels: 22.8 us -> 25.4 us
  starting transfers between devices: 29.5 us -> 27.5 us
  waiting for transfers between devices: 29.1 us -> 30.1 us
    pallas_call x1, Pallas kernels: 1.05 us -> 4.53 us  [body(): call(functools.partial(index_kernel, shards), [shape((GROUPS, rows, 16),...]
    ppermute x11, starting transfers between devices: 14.3 us -> 13.2 us  [swapped(): return lax.ppermute(shard, axis, [(0, 1), (1, 0)])]
    ppermute x8, waiting for transfers between devices: 21.4 us -> 22.3 us  [apart(): lax.ppermute(shard, 'curve', [(i, i ^ by) for i in range(lax.axis_size('c...]
  transfers between devices with their start and end apart: 25 -> 25, of which waited for: 9 -> 9; matrix products, arithmetic and copies ran while one was open for 3% -> 3% of each run, Pallas kernels for 11% -> 15%
where the time goes in v2:
time: 89 us; the launch traced here: 88.7 us
  waiting for transfers between devices  30.1 us (34%)
  starting transfers between devices  27.5 us (31%)
  Pallas kernels  25.4 us (29%)
  other arithmetic  2.46 us (3%)
  local copies, waits for them, and re-layouts  2.23 us (3%)
  between operations  1.06 us (1%)
    ppermute x8, waiting for transfers between devices, apart(): lax.ppermute(shard, 'curve', [(i, i ^ by) for i in range(lax.axis_size('c...  22.3 us
    ppermute x11, starting transfers between devices, swapped(): return lax.ppermute(shard, axis, [(0, 1), (1, 0)])  13.2 us
    pallas_call x1, Pallas kernels, body(): call(functools.partial(conv_kernel, chans, shards, scale), [shape((channe...  9.48 us
    ppermute x8, starting transfers between devices, apart(): lax.ppermute(shard, 'curve', [(i, i ^ by) for i in range(lax.axis_size('c...  8.69 us
    pallas_call x1, Pallas kernels, body(): call(coarse_grad_kernel, [shape((channels, rows), F32), shape((chans - 1,...  5.93 us
    ppermute x1, waiting for transfers between devices, body(): lax.ppermute(others[by - 1], 'chan', [(i, (i + by) % chans) for i in rang...  4.99 us
    pallas_call x1, Pallas kernels, body(): call(functools.partial(index_kernel, shards), [shape((GROUPS, rows, 16),...  4.53 us
    ppermute x11, waiting for transfers between devices, swapped(): return lax.ppermute(shard, axis, [(0, 1), (1, 0)])  2.74 us
  transfers between devices with their start and end apart: 25, of which 9 were waited for; matrix products, arithmetic and copies ran while one was open for 3% of the time, Pallas kernels for 15%

profile of v2, /device:TPU:0, one launch (start us, length us, event | category | flops | bytes accessed | tf_op | source)
XLA Modules:
  0.0 88.7 jit_solution(3679520053964285665)
XLA Ops:
  0.7 2.7 %shard_map.93 = (bf16[768,128]{1,0:T(8,128)(2,1)}, f32[128,768]{1,0:T(8,128)}) custom-call(bf16[8,128,768]{2,1,0:T(8,128)(2,1)} %children_ref.3, s32[8,768]{1,0:T(8,128)} %mask_ref.4, bf16[8,128,128]{2,1,0:T(8,128)(2,1)} %weight_ref.2), custom_call_target="tpu_custom_call" | custom-call | tf_op jit(solution)/shard_map/pallas_call | solution.py:351
  3.4 2.9 %collective-permute-start = (bf16[768,128]{1,0:T(8,128)(2,1)}, bf16[768,128]{1,0:T(8,128)(2,1)S(1)}, u32[]{:S(2)}, u32[]{:S(2)}) collective-permute-start(bf16[768,128]{1,0:T(8,128)(2,1)} %get-tuple-element.35.refs_0_), channel_id=1, source_target_pairs={{0,2},{2,0},{1,3},{3,1},{4,6},{6,4},{5,7},{7,5},{8,10},{10,8},{9,1... | collective-permute-start | bytes 589832 | tf_op jit(solution)/shard_map/ppermute | solution.py:37
  6.3 0.7 collective-permute-start.1
  7.0 3.0 %collective-permute-start.2 = (bf16[768,128]{1,0:T(8,128)(2,1)}, bf16[768,128]{1,0:T(8,128)(2,1)S(1)}, u32[]{:S(2)}, u32[]{:S(2)}) collective-permute-start(bf16[768,128]{1,0:T(8,128)(2,1)} %get-tuple-element.35.refs_0_), channel_id=1, source_target_pairs={{0,1},{1,0},{2,3},{3,2},{4,5},{5,4},{6,7},{7,6},{8,9},{9,8},{10,11... | collective-permute-start | bytes 589832 | tf_op jit(solution)/shard_map/ppermute | solution.py:37
  10.0 1.5 %collective-permute-done.refs_3_ = bf16[768,128]{1,0:T(8,128)(2,1)S(1)} collective-permute-done((bf16[768,128]{1,0:T(8,128)(2,1)}, bf16[768,128]{1,0:T(8,128)(2,1)S(1)}, u32[]{:S(2)}, u32[]{:S(2)}) %collective-permute-start) | collective-permute-done | bytes 196640 | tf_op jit(solution)/shard_map/ppermute | solution.py:37
  11.5 0.7 collective-permute-start.3
  12.2 3.2 %collective-permute-start.4 = (bf16[768,128]{1,0:T(8,128)(2,1)S(1)}, bf16[768,128]{1,0:T(8,128)(2,1)S(1)}, u32[]{:S(2)}, u32[]{:S(2)}) collective-permute-start(bf16[768,128]{1,0:T(8,128)(2,1)S(1)} %collective-permute-done.refs_3_), channel_id=1, source_target_pairs={{0,1},{1,0},{2,3},{3,2},{4,5},{5,4},{6,7},{7,6},{8,9},{9,8},{10,11... | collective-permute-start | bytes 589832 | tf_op jit(solution)/shard_map/ppermute | solution.py:37
  15.3 1.6 %broadcast_multiply_fusion.weight_ref = bf16[27,128,256]{2,1,0:T(8,128)(2,1)S(1)} fusion(bf16[27,128,256]{2,1,0:T(8,128)(2,1)} %param.10, bf16[]{:T(256)} %constant.3.clone.1), kind=kLoop, calls=%fused_computation | loop fusion | flops 884736 | bytes 3538946 | tf_op jit(solution)/shard_map/mul | solution.py:365
  17.0 4.5 %shard_map.94 = (s32[3,768,16]{2,1,0:T(8,128)S(1)}, s32[201]{0:T(256)S(1)}) custom-call(s32[27,768]{1,0:T(8,128)S(1)} %copy-done.6), custom_call_target="tpu_custom_call" | custom-call | tf_op jit(solution)/shard_map/pallas_call | solution.py:367
  21.6 9.5 %shard_map.95 = (bf16[128,768]{1,0:T(8,128)(2,1)}, bf16[768,128]{1,0:T(8,128)(2,1)S(1)}, bf16[4,27,16,256]{3,2,1,0:T(8,128)(2,1)S(1)}, bf16[4,27,16,256]{3,2,1,0:T(8,128)(2,1)S(1)}) custom-call(s32[201]{0:T(256)S(1)} %get-tuple-element.50.scalars_ref, s32[3,768,16]{2,1,0:T(8,128)S(1)} %get-tuple-element.38.index_ref, ...), custom_call_target="tpu_custom_call" | custom-call | tf_op jit(solution)/shard_map/pallas_call | solution.py:375
  31.1 0.8 collective-permute-start.6
  31.9 3.4 %collective-permute-start.7 = (bf16[768,128]{1,0:T(8,128)(2,1)S(1)}, bf16[768,128]{1,0:T(8,128)(2,1)S(1)}, u32[]{:S(2)}, u32[]{:S(2)}) collective-permute-start(bf16[768,128]{1,0:T(8,128)(2,1)S(1)} %get-tuple-element.44.refs_0_), channel_id=1, source_target_pairs={{0,1},{1,0},{2,3},{3,2},{4,5},{5,4},{6,7},{7,6},{8,9},{9,8},{10,11... | collective-permute-start | bytes 589832 | tf_op jit(solution)/shard_map/ppermute | solution.py:37
  35.6 1.6 %collective-permute-start.11 = (bf16[27,16,256]{2,1,0:T(8,128)(2,1)S(1)}, bf16[27,16,256]{2,1,0:T(8,128)(2,1)S(1)}, u32[]{:S(2)}, u32[]{:S(2)}) collective-permute-start(bf16[27,16,256]{2,1,0:T(8,128)(2,1)S(1)} %get-tuple-element.70), channel_id=1, source_target_pairs={{0,4},{4,0},{8,12},{12,8},{1,5},{5,1},{9,13},{13,9},{2,6},{6,2},{1... | collective-permute-start | bytes 663560 | tf_op jit(solution)/shard_map/ppermute | solution.py:325
  37.2 1.6 %collective-permute-start.10 = (bf16[27,16,256]{2,1,0:T(8,128)(2,1)S(1)}, bf16[27,16,256]{2,1,0:T(8,128)(2,1)S(1)}, u32[]{:S(2)}, u32[]{:S(2)}) collective-permute-start(bf16[27,16,256]{2,1,0:T(8,128)(2,1)S(1)} %get-tuple-element.58), channel_id=1, source_target_pairs={{0,12},{4,8},{8,4},{12,0},{1,13},{5,9},{9,5},{13,1},{2,14},{6,10},... | collective-permute-start | bytes 663560 | tf_op jit(solution)/shard_map/ppermute | solution.py:325
  38.8 0.6 collective-permute-start.9
  39.5 5.9 %shard_map.96 = (f32[128,768]{1,0:T(8,128)S(1)}, bf16[1,128,768]{2,1,0:T(8,128)(2,1)S(1)}) custom-call(s32[201]{0:T(256)S(1)} %get-tuple-element.50.scalars_ref, s32[3,768,16]{2,1,0:T(8,128)S(1)} %get-tuple-element.38.index_ref, bf16[27,128,256]{2,1,0:T(8,128)(2,1)S(1)} %broadcast_multiply_fusion.weight_ref, bf16[768,128]{1,0:T(8,128)(2,1)S(1)} %get-tuple-element.44.refs_0_, ...), custom_call_target="tpu_custom_call" | custom-call | tf_op jit(solution)/shard_map/pallas_call | solution.py:400
  45.4 1.6 %collective-permute-start.8 = (bf16[128,768]{1,0:T(8,128)(2,1)S(1)}, bf16[128,768]{1,0:T(8,128)(2,1)S(1)}, u32[]{:S(2)}, u32[]{:S(2)}) collective-permute-start(bf16[128,768]{1,0:T(8,128)(2,1)S(1)} %bitcast.9), channel_id=1, source_target_pairs={{0,2},{2,0},{1,3},{3,1},{4,6},{6,4},{5,7},{7,5},{8,10},{10,8},{9,1... | collective-permute-start | bytes 589832 | tf_op jit(solution)/shard_map/ppermute | solution.py:411
  47.1 5.0 %collective-permute-done.8.refs_0_ = bf16[128,768]{1,0:T(8,128)(2,1)S(1)} collective-permute-done((bf16[128,768]{1,0:T(8,128)(2,1)S(1)}, bf16[128,768]{1,0:T(8,128)(2,1)S(1)}, u32[]{:S(2)}, u32[]{:S(2)}) %collective-permute-start.8) | collective-permute-done | bytes 196640 | tf_op jit(solution)/shard_map/ppermute | solution.py:411
  52.1 1.2 %shard_map.98 = (bf16[128,768]{1,0:T(8,128)(2,1)S(1)}, bf16[8,64,128]{2,1,0:T(8,128)(2,1)S(1)}, bf16[8,64,128]{2,1,0:T(8,128)(2,1)S(1)}) custom-call(s32[201]{0:T(256)S(1)} %get-tuple-element.50.scalars_ref, bf16[8,128,768]{2,1,0:T(8,128)(2,1)S(1)} %copy-done, s32[8,768]{1,0:T(8,128)S(1)} %copy-done.3, f32[128,768]{1,0:T(8,128)S(1)} %copy-done.2, ...), custom_call_target="tpu_custom_call" | custom-call | tf_op jit(solution)/shard_map/pallas_call | solution.py:425
  53.4 6.0 %collective-permute-done.9 = bf16[27,16,256]{2,1,0:T(8,128)(2,1)S(1)} collective-permute-done((bf16[27,16,256]{2,1,0:T(8,128)(2,1)S(1)}, bf16[27,16,256]{2,1,0:T(8,128)(2,1)S(1)}, u32[]{:S(2)}, u32[]{:S(2)}) %collective-permute-start.9) | collective-permute-done | bytes 221216 | tf_op jit(solution)/shard_map/ppermute | solution.py:325
  60.0 2.3 %collective-permute-start.19 = (bf16[27,16,256]{2,1,0:T(8,128)(2,1)S(1)}, bf16[27,16,256]{2,1,0:T(8,128)(2,1)S(1)}, u32[]{:S(2)}, u32[]{:S(2)}) collective-permute-start(bf16[27,16,256]{2,1,0:T(8,128)(2,1)S(1)} %add_convert_fusion), channel_id=1, source_target_pairs={{0,8},{4,12},{8,0},{12,4},{1,9},{5,13},{9,1},{13,5},{2,10},{6,14},... | collective-permute-start | bytes 663560 | tf_op jit(solution)/shard_map/ppermute | solution.py:325
  62.4 1.5 %collective-permute-start.14 = (bf16[128,768]{1,0:T(8,128)(2,1)S(1)}, bf16[128,768]{1,0:T(8,128)(2,1)S(1)}, u32[]{:S(2)}, u32[]{:S(2)}) collective-permute-start(bf16[128,768]{1,0:T(8,128)(2,1)S(1)} %get-tuple-element.61.refs_0_), channel_id=1, source_target_pairs={{0,2},{2,0},{1,3},{3,1},{4,6},{6,4},{5,7},{7,5},{8,10},{10,8},{9,1... | collective-permute-start | bytes 589832 | tf_op jit(solution)/shard_map/ppermute | solution.py:442
  65.0 7.5 %collective-permute-done.17 = bf16[27,16,256]{2,1,0:T(8,128)(2,1)S(1)} collective-permute-done((bf16[27,16,256]{2,1,0:T(8,128)(2,1)S(1)}, bf16[27,16,256]{2,1,0:T(8,128)(2,1)S(1)}, u32[]{:S(2)}, u32[]{:S(2)}) %collective-permute-start.17) | collective-permute-done | bytes 221216 | tf_op jit(solution)/shard_map/ppermute | solution.py:325
  72.5 0.8 collective-permute-done.19
  73.4 1.7 %collective-permute-done.13 = bf16[8,64,128]{2,1,0:T(8,128)(2,1)S(1)} collective-permute-done((bf16[8,64,128]{2,1,0:T(8,128)(2,1)S(1)}, bf16[8,64,128]{2,1,0:T(8,128)(2,1)S(1)}, u32[]{:S(2)}, u32[]{:S(2)}) %collective-permute-start.13) | collective-permute-done | bytes 131104 | tf_op jit(solution)/shard_map/ppermute | solution.py:325
  75.1 0.7 collective-permute-start.23
  75.8 1.8 %collective-permute-start.21 = (bf16[27,16,256]{2,1,0:T(8,128)(2,1)S(1)}, bf16[27,16,256]{2,1,0:T(8,128)(2,1)S(1)}, u32[]{:S(2)}, u32[]{:S(2)}) collective-permute-start(bf16[27,16,256]{2,1,0:T(8,128)(2,1)S(1)} %collective-permute-done.19), channel_id=1, source_target_pairs={{0,4},{4,0},{8,12},{12,8},{1,5},{5,1},{9,13},{13,9},{2,6},{6,2},{1... | collective-permute-start | bytes 663560 | tf_op jit(solution)/shard_map/ppermute | solution.py:325
  77.6 1.3 %shard_map.99 = bf16[8,64,768]{2,1,0:T(8,128)(2,1)} custom-call(s32[8,768]{1,0:T(8,128)S(1)} %copy-done.3, bf16[128,768]{1,0:T(8,128)(2,1)S(1)} %get-tuple-element.61.refs_0_, bf16[128,768]{1,0:T(8,128)(2,1)S(1)} %collective-permute-done.14.refs_1_, bf16[8,64,128]{2,1,0:T(8,128)(2,1)S(1)} %get-tuple-element.47.refs_2_, ...), custom_call_target="tpu_custom_call" | custom-call | tf_op jit(solution)/shard_map/pallas_call | solution.py:462
  78.9 4.8 %collective-permute-done.23 = bf16[8,64,128]{2,1,0:T(8,128)(2,1)S(1)} collective-permute-done((bf16[8,64,128]{2,1,0:T(8,128)(2,1)S(1)}, bf16[8,64,128]{2,1,0:T(8,128)(2,1)S(1)}, u32[]{:S(2)}, u32[]{:S(2)}) %collective-permute-start.23) | collective-permute-done | bytes 131104 | tf_op jit(solution)/shard_map/ppermute | solution.py:325
  83.9 1.5 %collective-permute-done.21 = bf16[27,16,256]{2,1,0:T(8,128)(2,1)S(1)} collective-permute-done((bf16[27,16,256]{2,1,0:T(8,128)(2,1)S(1)}, bf16[27,16,256]{2,1,0:T(8,128)(2,1)S(1)}, u32[]{:S(2)}, u32[]{:S(2)}) %collective-permute-start.21) | collective-permute-done | bytes 221216 | tf_op jit(solution)/shard_map/ppermute | solution.py:325
  85.7 1.2 %collective-permute-done.22 = bf16[27,16,256]{2,1,0:T(8,128)(2,1)S(1)} collective-permute-done((bf16[27,16,256]{2,1,0:T(8,128)(2,1)S(1)}, bf16[27,16,256]{2,1,0:T(8,128)(2,1)S(1)}, u32[]{:S(2)}, u32[]{:S(2)}) %collective-permute-start.22) | collective-permute-done | bytes 221216 | tf_op jit(solution)/shard_map/ppermute | solution.py:37
  87.0 1.8 %copy-done.7 = f32[27,128,256]{2,1,0:T(8,128)} copy-done((f32[27,128,256]{2,1,0:T(8,128)}, f32[27,128,256]{2,1,0:T(8,128)S(1)}, u32[]{:S(2)}) %copy-start.7) | copy-done | bytes 3538968
  (60 shorter events, 2.8 us)
Async XLA Ops:
  0.6 16.3 %copy-start.6 = (s32[27,768]{1,0:T(8,128)S(1)}, s32[27,768]{1,0:T(8,128)}, u32[]{:S(2)}) copy-start(s32[27,768]{1,0:T(8,128)} %neighbours_ref) | copy-start | bytes 248836
  0.6 20.9 %copy-start.4 = (bf16[128,768]{1,0:T(8,128)(2,1)S(1)}, bf16[128,768]{1,0:T(8,128)(2,1)}, u32[]{:S(2)}) copy-start(bf16[128,768]{1,0:T(8,128)(2,1)} %cotangent_ref.1) | copy-start | bytes 589828
  3.4 18.2 %copy-start.5 = (bf16[768,128]{1,0:T(8,128)(2,1)S(1)}, bf16[768,128]{1,0:T(8,128)(2,1)}, u32[]{:S(2)}) copy-start(bf16[768,128]{1,0:T(8,128)(2,1)} %get-tuple-element.35.refs_0_) | copy-start | bytes 589828
  3.4 8.1 %collective-permute-start = (bf16[768,128]{1,0:T(8,128)(2,1)}, bf16[768,128]{1,0:T(8,128)(2,1)S(1)}, u32[]{:S(2)}, u32[]{:S(2)}) collective-permute-start(bf16[768,128]{1,0:T(8,128)(2,1)} %get-tuple-element.35.refs_0_), channel_id=1, source_target_pairs={{0,2},{2,0},{1,3},{3,1},{4,6},{6,4},{5,7},{7,5},{8,10},{10,8},{9,1... | collective-permute-start | bytes 589832 | tf_op jit(solution)/shard_map/ppermute | solution.py:37
  6.3 15.2 %collective-permute-start.1 = (bf16[768,128]{1,0:T(8,128)(2,1)}, bf16[768,128]{1,0:T(8,128)(2,1)S(1)}, u32[]{:S(2)}, u32[]{:S(2)}) collective-permute-start(bf16[768,128]{1,0:T(8,128)(2,1)} %get-tuple-element.35.refs_0_), channel_id=1, source_target_pairs={{1,4},{5,8},{9,12},{4,1},{8,5},{12,9},{3,6},{7,10},{11,14},{6,3},{... | collective-permute-start | bytes 589832 | tf_op jit(solution)/shard_map/ppermute | solution.py:33
  7.0 14.5 %collective-permute-start.2 = (bf16[768,128]{1,0:T(8,128)(2,1)}, bf16[768,128]{1,0:T(8,128)(2,1)S(1)}, u32[]{:S(2)}, u32[]{:S(2)}) collective-permute-start(bf16[768,128]{1,0:T(8,128)(2,1)} %get-tuple-element.35.refs_0_), channel_id=1, source_target_pairs={{0,1},{1,0},{2,3},{3,2},{4,5},{5,4},{6,7},{7,6},{8,9},{9,8},{10,11... | collective-permute-start | bytes 589832 | tf_op jit(solution)/shard_map/ppermute | solution.py:37
  11.5 10.0 %collective-permute-start.3 = (bf16[768,128]{1,0:T(8,128)(2,1)S(1)}, bf16[768,128]{1,0:T(8,128)(2,1)S(1)}, u32[]{:S(2)}, u32[]{:S(2)}) collective-permute-start(bf16[768,128]{1,0:T(8,128)(2,1)S(1)} %collective-permute-done.refs_3_), channel_id=1, source_target_pairs={{1,4},{5,8},{9,12},{4,1},{8,5},{12,9},{3,6},{7,10},{11,14},{6,3},{... | collective-permute-start | bytes 589832 | tf_op jit(solution)/shard_map/ppermute | solution.py:33
  12.2 9.3 %collective-permute-start.4 = (bf16[768,128]{1,0:T(8,128)(2,1)S(1)}, bf16[768,128]{1,0:T(8,128)(2,1)S(1)}, u32[]{:S(2)}, u32[]{:S(2)}) collective-permute-start(bf16[768,128]{1,0:T(8,128)(2,1)S(1)} %collective-permute-done.refs_3_), channel_id=1, source_target_pairs={{0,1},{1,0},{2,3},{3,2},{4,5},{5,4},{6,7},{7,6},{8,9},{9,8},{10,11... | collective-permute-start | bytes 589832 | tf_op jit(solution)/shard_map/ppermute | solution.py:37
  31.0 15.9 %copy-start.1 = (bf16[8,128,128]{2,1,0:T(8,128)(2,1)S(1)}, bf16[8,128,128]{2,1,0:T(8,128)(2,1)}, u32[]{:S(2)}) copy-start(bf16[8,128,128]{2,1,0:T(8,128)(2,1)} %weight_ref.2) | copy-start | bytes 786436
  31.0 21.1 %copy-start = (bf16[8,128,768]{2,1,0:T(8,128)(2,1)S(1)}, bf16[8,128,768]{2,1,0:T(8,128)(2,1)}, u32[]{:S(2)}) copy-start(bf16[8,128,768]{2,1,0:T(8,128)(2,1)} %children_ref.3) | copy-start | bytes 4718596
  31.0 21.1 %copy-start.2 = (f32[128,768]{1,0:T(8,128)S(1)}, f32[128,768]{1,0:T(8,128)}, u32[]{:S(2)}) copy-start(f32[128,768]{1,0:T(8,128)} %get-tuple-element.51.slope_ref) | copy-start | bytes 1179652
  31.0 21.1 %copy-start.3 = (s32[8,768]{1,0:T(8,128)S(1)}, s32[8,768]{1,0:T(8,128)}, u32[]{:S(2)}) copy-start(s32[8,768]{1,0:T(8,128)} %mask_ref.4) | copy-start | bytes 73732
  31.0 4.3 %collective-permute-start.5 = (bf16[4,27,16,256]{3,2,1,0:T(8,128)(2,1)S(1)}, bf16[4,27,16,256]{3,2,1,0:T(8,128)(2,1)S(1)}, u32[]{:S(2)}, u32[]{:S(2)}) collective-permute-start(bf16[4,27,16,256]{3,2,1,0:T(8,128)(2,1)S(1)} %get-tuple-element.42), channel_id=1, source_target_pairs={{0,1},{1,0},{2,3},{3,2},{4,5},{5,4},{6,7},{7,6},{8,9},{9,8},{10,11... | collective-permute-start | bytes 2654216 | tf_op jit(solution)/shard_map/ppermute | solution.py:37
  31.1 8.3 %collective-permute-start.6 = (bf16[768,128]{1,0:T(8,128)(2,1)S(1)}, bf16[768,128]{1,0:T(8,128)(2,1)S(1)}, u32[]{:S(2)}, u32[]{:S(2)}) collective-permute-start(bf16[768,128]{1,0:T(8,128)(2,1)S(1)} %get-tuple-element.44.refs_0_), channel_id=1, source_target_pairs={{1,4},{5,8},{9,12},{4,1},{8,5},{12,9},{3,6},{7,10},{11,14},{6,3},{... | collective-permute-start | bytes 589832 | tf_op jit(solution)/shard_map/ppermute | solution.py:33
  31.9 5.3 %collective-permute-start.7 = (bf16[768,128]{1,0:T(8,128)(2,1)S(1)}, bf16[768,128]{1,0:T(8,128)(2,1)S(1)}, u32[]{:S(2)}, u32[]{:S(2)}) collective-permute-start(bf16[768,128]{1,0:T(8,128)(2,1)S(1)} %get-tuple-element.44.refs_0_), channel_id=1, source_target_pairs={{0,1},{1,0},{2,3},{3,2},{4,5},{5,4},{6,7},{7,6},{8,9},{9,8},{10,11... | collective-permute-start | bytes 589832 | tf_op jit(solution)/shard_map/ppermute | solution.py:37
  35.6 17.8 %collective-permute-start.11 = (bf16[27,16,256]{2,1,0:T(8,128)(2,1)S(1)}, bf16[27,16,256]{2,1,0:T(8,128)(2,1)S(1)}, u32[]{:S(2)}, u32[]{:S(2)}) collective-permute-start(bf16[27,16,256]{2,1,0:T(8,128)(2,1)S(1)} %get-tuple-element.70), channel_id=1, source_target_pairs={{0,4},{4,0},{8,12},{12,8},{1,5},{5,1},{9,13},{13,9},{2,6},{6,2},{1... | collective-permute-start | bytes 663560 | tf_op jit(solution)/shard_map/ppermute | solution.py:325
  37.2 16.1 %collective-permute-start.10 = (bf16[27,16,256]{2,1,0:T(8,128)(2,1)S(1)}, bf16[27,16,256]{2,1,0:T(8,128)(2,1)S(1)}, u32[]{:S(2)}, u32[]{:S(2)}) collective-permute-start(bf16[27,16,256]{2,1,0:T(8,128)(2,1)S(1)} %get-tuple-element.58), channel_id=1, source_target_pairs={{0,12},{4,8},{8,4},{12,0},{1,13},{5,9},{9,5},{13,1},{2,14},{6,10},... | collective-permute-start | bytes 663560 | tf_op jit(solution)/shard_map/ppermute | solution.py:325
  38.8 20.5 %collective-permute-start.9 = (bf16[27,16,256]{2,1,0:T(8,128)(2,1)S(1)}, bf16[27,16,256]{2,1,0:T(8,128)(2,1)S(1)}, u32[]{:S(2)}, u32[]{:S(2)}) collective-permute-start(bf16[27,16,256]{2,1,0:T(8,128)(2,1)S(1)} %get-tuple-element.57), channel_id=1, source_target_pairs={{0,8},{4,12},{8,0},{12,4},{1,9},{5,13},{9,1},{13,5},{2,10},{6,14},... | collective-permute-start | bytes 663560 | tf_op jit(solution)/shard_map/ppermute | solution.py:325
  45.4 6.7 %collective-permute-start.8 = (bf16[128,768]{1,0:T(8,128)(2,1)S(1)}, bf16[128,768]{1,0:T(8,128)(2,1)S(1)}, u32[]{:S(2)}, u32[]{:S(2)}) collective-permute-start(bf16[128,768]{1,0:T(8,128)(2,1)S(1)} %bitcast.9), channel_id=1, source_target_pairs={{0,2},{2,0},{1,3},{3,1},{4,6},{6,4},{5,7},{7,5},{8,10},{10,8},{9,1... | collective-permute-start | bytes 589832 | tf_op jit(solution)/shard_map/ppermute | solution.py:411
  59.5 4.4 %collective-permute-start.12 = (bf16[8,64,128]{2,1,0:T(8,128)(2,1)S(1)}, bf16[8,64,128]{2,1,0:T(8,128)(2,1)S(1)}, u32[]{:S(2)}, u32[]{:S(2)}) collective-permute-start(bf16[8,64,128]{2,1,0:T(8,128)(2,1)S(1)} %get-tuple-element.59), channel_id=1, source_target_pairs={{0,1},{1,0},{2,3},{3,2},{4,5},{5,4},{6,7},{7,6},{8,9},{9,8},{10,11... | collective-permute-start | bytes 393224 | tf_op jit(solution)/shard_map/ppermute | solution.py:37
  59.6 5.3 %collective-permute-start.16 = (bf16[27,16,256]{2,1,0:T(8,128)(2,1)S(1)}, bf16[27,16,256]{2,1,0:T(8,128)(2,1)S(1)}, u32[]{:S(2)}, u32[]{:S(2)}) collective-permute-start(bf16[27,16,256]{2,1,0:T(8,128)(2,1)S(1)} %add_convert_fusion), channel_id=1, source_target_pairs={{0,1},{1,0},{2,3},{3,2},{4,5},{5,4},{6,7},{7,6},{8,9},{9,8},{10,11... | collective-permute-start | bytes 663560 | tf_op jit(solution)/shard_map/ppermute | solution.py:37
  60.0 12.4 %collective-permute-start.17 = (bf16[27,16,256]{2,1,0:T(8,128)(2,1)S(1)}, bf16[27,16,256]{2,1,0:T(8,128)(2,1)S(1)}, u32[]{:S(2)}, u32[]{:S(2)}) collective-permute-start(bf16[27,16,256]{2,1,0:T(8,128)(2,1)S(1)} %add_convert_fusion), channel_id=1, source_target_pairs={{0,4},{4,0},{8,12},{12,8},{1,5},{5,1},{9,13},{13,9},{2,6},{6,2},{1... | collective-permute-start | bytes 663560 | tf_op jit(solution)/shard_map/ppermute | solution.py:325
  60.0 13.3 %collective-permute-start.19 = (bf16[27,16,256]{2,1,0:T(8,128)(2,1)S(1)}, bf16[27,16,256]{2,1,0:T(8,128)(2,1)S(1)}, u32[]{:S(2)}, u32[]{:S(2)}) collective-permute-start(bf16[27,16,256]{2,1,0:T(8,128)(2,1)S(1)} %add_convert_fusion), channel_id=1, source_target_pairs={{0,8},{4,12},{8,0},{12,4},{1,9},{5,13},{9,1},{13,5},{2,10},{6,14},... | collective-permute-start | bytes 663560 | tf_op jit(solution)/shard_map/ppermute | solution.py:325
  62.4 15.3 %collective-permute-start.14 = (bf16[128,768]{1,0:T(8,128)(2,1)S(1)}, bf16[128,768]{1,0:T(8,128)(2,1)S(1)}, u32[]{:S(2)}, u32[]{:S(2)}) collective-permute-start(bf16[128,768]{1,0:T(8,128)(2,1)S(1)} %get-tuple-element.61.refs_0_), channel_id=1, source_target_pairs={{0,2},{2,0},{1,3},{3,1},{4,6},{6,4},{5,7},{7,5},{8,10},{10,8},{9,1... | collective-permute-start | bytes 589832 | tf_op jit(solution)/shard_map/ppermute | solution.py:442
  63.8 12.0 %collective-permute-start.15 = (bf16[8,64,128]{2,1,0:T(8,128)(2,1)S(1)}, bf16[8,64,128]{2,1,0:T(8,128)(2,1)S(1)}, u32[]{:S(2)}, u32[]{:S(2)}) collective-permute-start(bf16[8,64,128]{2,1,0:T(8,128)(2,1)S(1)} %get-tuple-element.62), channel_id=1, source_target_pairs={{0,2},{2,0},{1,3},{3,1},{4,6},{6,4},{5,7},{7,5},{8,10},{10,8},{9,1... | collective-permute-start | bytes 393224 | tf_op jit(solution)/shard_map/ppermute | solution.py:457
  64.9 10.2 %collective-permute-start.13 = (bf16[8,64,128]{2,1,0:T(8,128)(2,1)S(1)}, bf16[8,64,128]{2,1,0:T(8,128)(2,1)S(1)}, u32[]{:S(2)}, u32[]{:S(2)}) collective-permute-start(bf16[8,64,128]{2,1,0:T(8,128)(2,1)S(1)} %add_convert_fusion.7), channel_id=1, source_target_pairs={{0,4},{4,0},{8,12},{12,8},{1,5},{5,1},{9,13},{13,9},{2,6},{6,2},{1... | collective-permute-start | bytes 393224 | tf_op jit(solution)/shard_map/ppermute | solution.py:325
  72.5 12.9 %collective-permute-start.18 = (bf16[27,16,256]{2,1,0:T(8,128)(2,1)S(1)}, bf16[27,16,256]{2,1,0:T(8,128)(2,1)S(1)}, u32[]{:S(2)}, u32[]{:S(2)}) collective-permute-start(bf16[27,16,256]{2,1,0:T(8,128)(2,1)S(1)} %collective-permute-done.17), channel_id=1, source_target_pairs={{0,1},{1,0},{2,3},{3,2},{4,5},{5,4},{6,7},{7,6},{8,9},{9,8},{10,11... | collective-permute-start | bytes 663560 | tf_op jit(solution)/shard_map/ppermute | solution.py:37
  73.3 12.2 %collective-permute-start.20 = (bf16[27,16,256]{2,1,0:T(8,128)(2,1)S(1)}, bf16[27,16,256]{2,1,0:T(8,128)(2,1)S(1)}, u32[]{:S(2)}, u32[]{:S(2)}) collective-permute-start(bf16[27,16,256]{2,1,0:T(8,128)(2,1)S(1)} %collective-permute-done.19), channel_id=1, source_target_pairs={{0,1},{1,0},{2,3},{3,2},{4,5},{5,4},{6,7},{7,6},{8,9},{9,8},{10,11... | collective-permute-start | bytes 663560 | tf_op jit(solution)/shard_map/ppermute | solution.py:37
  75.1 8.6 %collective-permute-start.23 = (bf16[8,64,128]{2,1,0:T(8,128)(2,1)S(1)}, bf16[8,64,128]{2,1,0:T(8,128)(2,1)S(1)}, u32[]{:S(2)}, u32[]{:S(2)}) collective-permute-start(bf16[8,64,128]{2,1,0:T(8,128)(2,1)S(1)} %add_convert_fusion.6), channel_id=1, source_target_pairs={{0,8},{4,12},{8,0},{12,4},{1,9},{5,13},{9,1},{13,5},{2,10},{6,14},... | collective-permute-start | bytes 393224 | tf_op jit(solution)/shard_map/ppermute | solution.py:325
  75.8 9.6 %collective-permute-start.21 = (bf16[27,16,256]{2,1,0:T(8,128)(2,1)S(1)}, bf16[27,16,256]{2,1,0:T(8,128)(2,1)S(1)}, u32[]{:S(2)}, u32[]{:S(2)}) collective-permute-start(bf16[27,16,256]{2,1,0:T(8,128)(2,1)S(1)} %collective-permute-done.19), channel_id=1, source_target_pairs={{0,4},{4,0},{8,12},{12,8},{1,5},{5,1},{9,13},{13,9},{2,6},{6,2},{1... | collective-permute-start | bytes 663560 | tf_op jit(solution)/shard_map/ppermute | solution.py:325
  83.8 1.8 %collective-permute-start.24 = (bf16[8,64,128]{2,1,0:T(8,128)(2,1)S(1)}, bf16[8,64,128]{2,1,0:T(8,128)(2,1)S(1)}, u32[]{:S(2)}, u32[]{:S(2)}) collective-permute-start(bf16[8,64,128]{2,1,0:T(8,128)(2,1)S(1)} %get-tuple-element.67), channel_id=1, source_target_pairs={{0,1},{1,0},{2,3},{3,2},{4,5},{5,4},{6,7},{7,6},{8,9},{9,8},{10,11... | collective-permute-start | bytes 393224 | tf_op jit(solution)/shard_map/ppermute | solution.py:37
  85.4 1.5 %collective-permute-start.22 = (bf16[27,16,256]{2,1,0:T(8,128)(2,1)S(1)}, bf16[27,16,256]{2,1,0:T(8,128)(2,1)S(1)}, u32[]{:S(2)}, u32[]{:S(2)}) collective-permute-start(bf16[27,16,256]{2,1,0:T(8,128)(2,1)S(1)} %collective-permute-done.21), channel_id=1, source_target_pairs={{0,1},{1,0},{2,3},{3,2},{4,5},{5,4},{6,7},{7,6},{8,9},{9,8},{10,11... | collective-permute-start | bytes 663560 | tf_op jit(solution)/shard_map/ppermute | solution.py:37
  (2 other events, 3.1 us)
